TPU v7x, 32 devices: a whole 2x2x4 slice. The times are simulated.
32 devices in a mesh: cls: 8 (over y, x, core), slab: 4 (over z).
Axes of the slice: x: 2, y: 2, z: 4, core: 2. Of those that a mesh axis runs over, the one named last changes fastest.
Arguments:
- q_init: bfloat16 [32, 64, 64, 128], P('cls', 'slab'), may hold values from 0.5 to 2
- q_back: bfloat16 [32, 4, 64, 64, 128], P('cls', None, 'slab'), may hold values from 0.5 to 2
- fields: float32 [2, 64, 64, 128], P(None, 'slab'), may hold values from -4 to 4
- lengths: int32 [32], replicated, may hold values from 16 to 63
- steps_count: int32 [32], replicated, may hold values from 64 to 127
- block_types: int32 [32, 4], replicated, may hold values from 0 to 1
Outputs:
- fields_new: float32 [2, 64, 64, 128], P(None, 'slab')
- q_final: bfloat16 [32, 64, 64, 128], P('cls', 'slab')
Inputs may be any that keep to these rules, and one draw needn't show every extreme that they name: `steps_count`: steps of each class's whole chain.
All inputs are finite; a program needn't handle non-finite values.
Results may differ from a plain program's by a relative error of at most 0.001.
Values sent between devices are 32-bit elements; how exact they have to be, the bound alone decides.
A program may use at most 64 MiB of HBM per device.

v0:
```python
import jax
import jax.numpy as jnp
from jax import lax
from jax.sharding import PartitionSpec as P

flory_chi = 2.0
stiffness = 1.0
mixing = 0.5
diffusion_scale = 0.125


def padded_2(block, sides, width):
    for axis, dim in sides:
        count = lax.axis_size(axis)
        forward = [(i, i + 1) for i in range(count - 1)]
        backward = [(target, source) for source, target in forward]
        low = lax.ppermute(
            lax.slice_in_dim(block, block.shape[dim] - width, None, axis=dim), axis, forward
        )
        high = lax.ppermute(lax.slice_in_dim(block, 0, width, axis=dim), axis, backward)
        block = jnp.concatenate([low, block, high], axis=dim)
    return block


def column(values):
    return values[:, None, None, None]


def stencil_core(extended):
    core = extended[:, 1:-1]
    total = extended[:, 2:] + extended[:, :-2]
    padded = jnp.pad(core, ((0, 0), (0, 0), (1, 1), (1, 1)))
    total = total + padded[:, :, 2:, 1:-1] + padded[:, :, :-2, 1:-1]
    total = total + padded[:, :, 1:-1, 2:] + padded[:, :, 1:-1, :-2]
    return (core, total)


def update_fields(density, old_fields, level):
    total = density[0] + density[1]
    pressure = stiffness * (total - level)
    first = old_fields[0] + mixing * (flory_chi * density[1] + pressure - old_fields[0])
    second = old_fields[1] + mixing * (flory_chi * density[0] + pressure - old_fields[1])
    return jnp.stack([first, second])


def body(q_init, q_back, fields, lengths, steps_count, block_types):
    class_count = q_init.shape[0]
    planes = q_init.shape[1]
    width_x = q_init.shape[2]
    width_y = q_init.shape[3]
    depth = q_back.shape[1]
    cells = lax.axis_size("slab") * planes * width_x * width_y
    first_class = lax.axis_index("cls") * class_count
    size_all = lengths.astype(jnp.float32) / steps_count.astype(jnp.float32)
    share_all = lengths.astype(jnp.float32) / jnp.sum(lengths).astype(jnp.float32)
    step_size = lax.dynamic_slice_in_dim(size_all, first_class, class_count)
    fraction = lax.dynamic_slice_in_dim(share_all, first_class, class_count)
    types = lax.dynamic_slice_in_dim(block_types, first_class, class_count, 0)
    spread = diffusion_scale * step_size
    products = []
    forward = q_init.astype(jnp.float32)
    for step in range(depth):
        chosen = jnp.where(column(types[:, step] == 0), fields[0][None], fields[1][None])
        half = jnp.exp(-0.5 * column(step_size) * chosen)
        weighted = half * forward
        extended = padded_2(weighted, (("slab", 1),), 1)
        core, total = stencil_core(extended)
        forward = half * ((1.0 - 6.0 * column(spread)) * core + column(spread) * total)
        products.append(forward * q_back[:, step].astype(jnp.float32))
    local_part = jnp.sum(products[0], axis=(1, 2, 3))
    partition = lax.psum(local_part, "slab") / cells
    weight = fraction * step_size / partition
    density = jnp.zeros((2, planes, width_x, width_y), jnp.float32)
    for step in range(depth):
        select = (jnp.arange(2, dtype=jnp.int32)[None, :] == types[:, step : step + 1]).astype(
            jnp.float32
        )
        factor = weight[:, None] * select
        density = density + jnp.einsum(
            "ct,czxy->tzxy", factor, products[step], precision=lax.Precision.HIGHEST
        )
    whole = lax.psum(density, "cls")
    level = lax.psum(jnp.sum(whole[0] + whole[1]), "slab") / cells
    fields_new = update_fields(whole, fields, level)
    return (fields_new, forward.astype(jnp.bfloat16))


def solution(mesh):
    return jax.shard_map(
        body,
        mesh=mesh,
        in_specs=(
            P("cls", "slab", None, None),
            P("cls", None, "slab", None, None),
            P(None, "slab", None, None),
            P(),
            P(),
            P(),
        ),
        out_specs=(P(None, "slab", None, None), P("cls", "slab", None, None)),
        check_vma=False,
    )
```

profile of v0, /device:TPU:0, one launch (start us, length us, event | category | flops | bytes accessed | tf_op | source)
XLA Modules:
  0.0 166.4 jit_solution(15439202298060862239)
XLA Ops:
  7.2 0.0 copy-start
  7.2 0.0 copy-start.3
  7.2 0.0 all-reduce.6.cloned.1.call-start
  7.2 1.4 reduce_sum.27
  9.3 0.7 convert_divide_fusion.1
  9.9 0.1 multiply_subtract_fusion
  10.0 0.0 copy-done
  10.0 0.1 constant_dynamic-slice_fusion
  10.1 1.3 slice_bitcast_fusion.1
  11.4 0.0 copy-done.3
  11.4 0.5 convert_multiply_fusion.4
  11.9 1.3 collective-permute-start
  13.2 5.6 %collective-permute-start.1 = (f32[4,1,64,128]{3,2,1,0:T(8,128)S(1)}, f32[4,1,64,128]{3,2,1,0:T(8,128)S(1)}, u32[]{:S(2)}, u32[]{:S(2)}) collective-permute-start(f32[4,1,64,128]{3,2,1,0:T(8,128)S(1)} %get-tuple-element.24), channel_id=1, source_target_pairs={{0,1},{1,2},{2,3},{4,5},{5,6},{6,7},{8,9},{9,10},{10,11},{12,13},{... | collective-permute-start | bytes 393224 | tf_op jit(solution)/shard_map/ppermute | solution.py:17
  18.8 1.5 collective-permute-done
  20.4 1.2 collective-permute-done.1
  21.5 4.4 %fusion.76 = (f32[4]{0:T(128)S(1)}, f32[4,16,64,128]{3,2,1,0:T(8,128)S(1)}, f32[4,16,64,128]{3,2,1,0:T(8,128)}) fusion(bf16[4,4,16,64,128]{4,3,2,1,0:T(8,128)(2,1)} %param.7, f32[4,16,64,128]{3,2,1,0:T(8,128)S(1)} %convert_multiply_fusion.4, f32[4,1,64,128]{3,2,1,0:T(8,128)S(1)} %collective-permute-done.1, f32[4,1,64,128]{3,2,1,0:T(8,128)S(1)} %collective-permute-done, ...), kind=kLoop, calls=%fused_computation.130 | loop fusion | flops 8388604 | bytes 8650820 | tf_op jit(solution)/shard_map/reduce_sum | solution.py:70
  26.0 13.0 %psum.21 = f32[4]{0:T(128)S(1)} all-reduce(f32[4]{0:T(128)S(1)} %get-tuple-element.10), channel_id=1, replica_groups=mesh['cls'=8,'slab'=4] {'slab'}, use_global_device_ids=true, to_apply=%region_2.3 | all-reduce | flops 4 | bytes 32 | tf_op jit(solution)/shard_map/psum | solution.py:71
  39.0 0.0 copy-start.1
  39.0 2.2 %fusion.42 = f32[4,16,64,128]{3,2,1,0:T(8,128)S(1)} fusion(f32[4,16,64,128]{3,2,1,0:T(8,128)} %get-tuple-element.12, f32[16,64,128]{2,1,0:T(8,128)S(1)} %get-tuple-element.26, f32[16,64,128]{2,1,0:T(8,128)S(1)} %get-tuple-element.25, f32[4]{0:T(128)S(1)} %get-tuple-element.38, pred[4]{0:T(512)(128)(4,1)S(1)} %get-tuple-element.33), kind=kLoop, calls=%fused_computation.73 | loop fusion | flops 1572864 | bytes 5242900 | tf_op jit(solution)/shard_map/mul | solution.py:65
  41.2 1.3 collective-permute-start.2
  42.5 4.6 %collective-permute-start.3 = (f32[4,1,64,128]{3,2,1,0:T(8,128)S(1)}, f32[4,1,64,128]{3,2,1,0:T(8,128)S(1)}, u32[]{:S(2)}, u32[]{:S(2)}) collective-permute-start(f32[4,1,64,128]{3,2,1,0:T(8,128)S(1)} %get-tuple-element.22), channel_id=1, source_target_pairs={{0,1},{1,2},{2,3},{4,5},{5,6},{6,7},{8,9},{9,10},{10,11},{12,13},{... | collective-permute-start | bytes 393224 | tf_op jit(solution)/shard_map/ppermute | solution.py:17
  47.1 0.1 multiply_divide_fusion
  47.2 4.3 %fusion.38 = f32[2,16,64,128]{3,0,2,1:T(2,128)S(1)} fusion(f32[4,16,64,128]{3,2,1,0:T(8,128)S(1)} %get-tuple-element.11, f32[4]{0:T(128)S(1)} %multiply_divide_fusion, s32[4]{0:T(128)S(1)} %get-tuple-element.27), kind=kOutput, calls=%fused_computation.66 | convolution fusion | flops 12582928 | bytes 3145760 | tf_op jit(solution)/shard_map/ct,czxy->tzxy/dot_general | solution.py:79
  51.5 0.0 collective-permute-done.2
  51.5 0.0 collective-permute-done.3
  51.5 0.0 copy-done.1
  51.5 2.6 %convert_multiply_fusion.2 = (f32[4,16,64,128]{3,2,1,0:T(8,128)S(1)}, f32[4,16,64,128]{3,2,1,0:T(8,128)S(1)}) fusion(bf16[4,4,16,64,128]{4,3,2,1,0:T(8,128)(2,1)S(1)} %copy-done.1, f32[4,16,64,128]{3,2,1,0:T(8,128)S(1)} %fusion.42, f32[4,1,64,128]{3,2,1,0:T(8,128)S(1)} %collective-permute-done.3, f32[4,1,64,128]{3,2,1,0:T(8,128)S(1)} %collective-permute-done.2, ...), kind=kLoop, calls=%fused_computation.58 | loop fusion | flops 7864320 | bytes 8650804 | tf_op jit(solution)/shard_map/mul | solution.py:69
  54.1 0.5 fusion.41
  54.7 1.3 collective-permute-start.4
  56.0 4.6 %collective-permute-start.5 = (f32[4,1,64,128]{3,2,1,0:T(8,128)S(1)}, f32[4,1,64,128]{3,2,1,0:T(8,128)S(1)}, u32[]{:S(2)}, u32[]{:S(2)}) collective-permute-start(f32[4,1,64,128]{3,2,1,0:T(8,128)S(1)} %get-tuple-element.20), channel_id=1, source_target_pairs={{0,1},{1,2},{2,3},{4,5},{5,6},{6,7},{8,9},{9,10},{10,11},{12,13},{... | collective-permute-start | bytes 393224 | tf_op jit(solution)/shard_map/ppermute | solution.py:17
  60.6 4.3 %fusion.36 = f32[2,16,64,128]{3,0,2,1:T(2,128)S(1)} fusion(f32[4,16,64,128]{3,2,1,0:T(8,128)S(1)} %get-tuple-element.6, s32[4]{0:T(128)S(1)} %get-tuple-element.30, f32[4]{0:T(128)S(1)} %multiply_divide_fusion), kind=kOutput, calls=%fused_computation.64 | convolution fusion | flops 12582928 | bytes 3145760 | tf_op jit(solution)/shard_map/ct,czxy->tzxy/dot_general | solution.py:79
  64.9 0.0 collective-permute-done.4
  64.9 0.0 collective-permute-done.5
  64.9 2.6 %convert_multiply_fusion.1 = (f32[4,16,64,128]{3,2,1,0:T(8,128)S(1)}, f32[4,16,64,128]{3,2,1,0:T(8,128)S(1)}) fusion(bf16[4,4,16,64,128]{4,3,2,1,0:T(8,128)(2,1)S(1)} %copy-done.1, f32[4,16,64,128]{3,2,1,0:T(8,128)S(1)} %fusion.41, f32[4,1,64,128]{3,2,1,0:T(8,128)S(1)} %collective-permute-done.5, f32[4,1,64,128]{3,2,1,0:T(8,128)S(1)} %collective-permute-done.4, ...), kind=kLoop, calls=%fused_computation.57 | loop fusion | flops 7864320 | bytes 8650804 | tf_op jit(solution)/shard_map/mul | solution.py:69
  67.5 0.4 fusion.40
  68.0 1.3 collective-permute-start.6
  69.3 4.7 %collective-permute-start.7 = (f32[4,1,64,128]{3,2,1,0:T(8,128)S(1)}, f32[4,1,64,128]{3,2,1,0:T(8,128)S(1)}, u32[]{:S(2)}, u32[]{:S(2)}) collective-permute-start(f32[4,1,64,128]{3,2,1,0:T(8,128)S(1)} %get-tuple-element.18), channel_id=1, source_target_pairs={{0,1},{1,2},{2,3},{4,5},{5,6},{6,7},{8,9},{9,10},{10,11},{12,13},{... | collective-permute-start | bytes 393224 | tf_op jit(solution)/shard_map/ppermute | solution.py:17
  74.0 4.3 %fusion.34 = f32[2,16,64,128]{3,0,2,1:T(2,128)S(1)} fusion(f32[4,16,64,128]{3,2,1,0:T(8,128)S(1)} %get-tuple-element.8, s32[4]{0:T(128)S(1)} %get-tuple-element.29, f32[4]{0:T(128)S(1)} %multiply_divide_fusion), kind=kOutput, calls=%fused_computation.62 | convolution fusion | flops 12582928 | bytes 3145760 | tf_op jit(solution)/shard_map/ct,czxy->tzxy/dot_general | solution.py:79
  78.3 0.0 collective-permute-done.6
  78.3 0.0 collective-permute-done.7
  78.3 3.0 %fusion.72 = (bf16[4,16,64,128]{3,2,1,0:T(8,128)(2,1)}, f32[4,16,64,128]{3,2,1,0:T(8,128)S(1)}) fusion(f32[4,16,64,128]{3,2,1,0:T(8,128)S(1)} %fusion.40, f32[4,1,64,128]{3,2,1,0:T(8,128)S(1)} %collective-permute-done.7, f32[4,1,64,128]{3,2,1,0:T(8,128)S(1)} %collective-permute-done.6, f32[4]{0:T(128)S(1)} %get-tuple-element.37, ...), kind=kLoop, calls=%fused_computation.129 | loop fusion | flops 7340032 | bytes 6553652 | tf_op jit(solution)/shard_map/convert_element_type | solution.py:85
  81.3 0.3 convert_multiply_fusion
  81.6 4.3 %fusion.32 = f32[2,16,64,128]{3,0,2,1:T(2,128)S(1)} fusion(f32[4,16,64,128]{3,2,1,0:T(8,128)S(1)} %convert_multiply_fusion, s32[4]{0:T(128)S(1)} %get-tuple-element.28, f32[4]{0:T(128)S(1)} %multiply_divide_fusion), kind=kOutput, calls=%fused_computation.60 | convolution fusion | flops 12582928 | bytes 3145760 | tf_op jit(solution)/shard_map/ct,czxy->tzxy/dot_general | solution.py:79
  85.9 1.3 copy_add_fusion
  87.2 0.0 copy-start.2
  87.2 0.0 all-reduce.6.cloned.1.call-update
  87.2 55.0 %all-reduce.6.cloned.1.call-done = f32[2,16,64,128]{3,2,1,0:T(8,128)} async-done(((f32[2,16,64,128]{3,2,1,0:T(8,128)}), f32[2,16,64,128]{3,2,1,0:T(8,128)}) %all-reduce.6.cloned.1.call-update) | async-done | bytes 1048592 | tf_op jit(solution)/shard_map/psum | solution.py:82
  142.2 1.9 %fusion.71 = f32[]{:T(128)} fusion(f32[2,16,64,128]{3,2,1,0:T(8,128)} %all-reduce.6.cloned.1.call-done), kind=kLoop, calls=%fused_computation.128 | loop fusion | flops 262143 | bytes 1048580 | tf_op jit(solution)/shard_map/reduce_sum | solution.py:83
  144.2 12.1 %psum.23 = f32[]{:T(128)} all-reduce(f32[]{:T(128)} %fusion.71), channel_id=1, replica_groups=mesh['cls'=8,'slab'=4] {'slab'}, use_global_device_ids=true, to_apply=%region_5.6 | all-reduce | flops 1 | bytes 8 | tf_op jit(solution)/shard_map/psum | solution.py:83
  157.0 0.0 copy-done.2
  157.0 1.5 multiply_add_fusion.1
  158.5 1.0 pad_maximum_fusion.8
  (7 shorter events, 0.1 us)
Async XLA Ops:
  7.2 2.9 %copy-start = (s32[32,4]{0,1:T(4,128)S(1)}, s32[32,4]{0,1:T(4,128)}, u32[]{:S(2)}) copy-start(s32[32,4]{0,1:T(4,128)} %param.11) | copy-start | bytes 1540
  7.2 4.2 %copy-start.3 = (bf16[4,16,64,128]{3,2,1,0:T(8,128)(2,1)S(1)}, bf16[4,16,64,128]{3,2,1,0:T(8,128)(2,1)}, u32[]{:S(2)}) copy-start(bf16[4,16,64,128]{3,2,1,0:T(8,128)(2,1)} %param.6) | copy-start | bytes 3145732
  7.2 135.1 %all-reduce.6.cloned.1.call-start = ((), (), s32[]{:S(2)}) async-start(), calls=%async_computation | async-start | bytes 2097152 | tf_op jit(solution)/shard_map/psum | solution.py:82
  11.9 8.4 %collective-permute-start = (f32[4,1,64,128]{3,2,1,0:T(8,128)S(1)}, f32[4,1,64,128]{3,2,1,0:T(8,128)S(1)}, u32[]{:S(2)}, u32[]{:S(2)}) collective-permute-start(f32[4,1,64,128]{3,2,1,0:T(8,128)S(1)} %get-tuple-element.23), channel_id=1, source_target_pairs={{1,0},{2,1},{3,2},{5,4},{6,5},{7,6},{9,8},{10,9},{11,10},{13,12},{... | collective-permute-start | bytes 393224 | tf_op jit(solution)/shard_map/ppermute | solution.py:20
  13.2 8.3 %collective-permute-start.1 = (f32[4,1,64,128]{3,2,1,0:T(8,128)S(1)}, f32[4,1,64,128]{3,2,1,0:T(8,128)S(1)}, u32[]{:S(2)}, u32[]{:S(2)}) collective-permute-start(f32[4,1,64,128]{3,2,1,0:T(8,128)S(1)} %get-tuple-element.24), channel_id=1, source_target_pairs={{0,1},{1,2},{2,3},{4,5},{5,6},{6,7},{8,9},{9,10},{10,11},{12,13},{... | collective-permute-start | bytes 393224 | tf_op jit(solution)/shard_map/ppermute | solution.py:17
  39.0 12.5 %copy-start.1 = (bf16[4,4,16,64,128]{4,3,2,1,0:T(8,128)(2,1)S(1)}, bf16[4,4,16,64,128]{4,3,2,1,0:T(8,128)(2,1)}, u32[]{:S(2)}) copy-start(bf16[4,4,16,64,128]{4,3,2,1,0:T(8,128)(2,1)} %param.7) | copy-start | bytes 12582916
  41.2 10.2 %collective-permute-start.2 = (f32[4,1,64,128]{3,2,1,0:T(8,128)S(1)}, f32[4,1,64,128]{3,2,1,0:T(8,128)S(1)}, u32[]{:S(2)}, u32[]{:S(2)}) collective-permute-start(f32[4,1,64,128]{3,2,1,0:T(8,128)S(1)} %get-tuple-element.21), channel_id=1, source_target_pairs={{1,0},{2,1},{3,2},{5,4},{6,5},{7,6},{9,8},{10,9},{11,10},{13,12},{... | collective-permute-start | bytes 393224 | tf_op jit(solution)/shard_map/ppermute | solution.py:20
  42.5 8.9 %collective-permute-start.3 = (f32[4,1,64,128]{3,2,1,0:T(8,128)S(1)}, f32[4,1,64,128]{3,2,1,0:T(8,128)S(1)}, u32[]{:S(2)}, u32[]{:S(2)}) collective-permute-start(f32[4,1,64,128]{3,2,1,0:T(8,128)S(1)} %get-tuple-element.22), channel_id=1, source_target_pairs={{0,1},{1,2},{2,3},{4,5},{5,6},{6,7},{8,9},{9,10},{10,11},{12,13},{... | collective-permute-start | bytes 393224 | tf_op jit(solution)/shard_map/ppermute | solution.py:17
  54.7 10.2 %collective-permute-start.4 = (f32[4,1,64,128]{3,2,1,0:T(8,128)S(1)}, f32[4,1,64,128]{3,2,1,0:T(8,128)S(1)}, u32[]{:S(2)}, u32[]{:S(2)}) collective-permute-start(f32[4,1,64,128]{3,2,1,0:T(8,128)S(1)} %get-tuple-element.19), channel_id=1, source_target_pairs={{1,0},{2,1},{3,2},{5,4},{6,5},{7,6},{9,8},{10,9},{11,10},{13,12},{... | collective-permute-start | bytes 393224 | tf_op jit(solution)/shard_map/ppermute | solution.py:20
  56.0 8.9 %collective-permute-start.5 = (f32[4,1,64,128]{3,2,1,0:T(8,128)S(1)}, f32[4,1,64,128]{3,2,1,0:T(8,128)S(1)}, u32[]{:S(2)}, u32[]{:S(2)}) collective-permute-start(f32[4,1,64,128]{3,2,1,0:T(8,128)S(1)} %get-tuple-element.20), channel_id=1, source_target_pairs={{0,1},{1,2},{2,3},{4,5},{5,6},{6,7},{8,9},{9,10},{10,11},{12,13},{... | collective-permute-start | bytes 393224 | tf_op jit(solution)/shard_map/ppermute | solution.py:17
  68.0 10.3 %collective-permute-start.6 = (f32[4,1,64,128]{3,2,1,0:T(8,128)S(1)}, f32[4,1,64,128]{3,2,1,0:T(8,128)S(1)}, u32[]{:S(2)}, u32[]{:S(2)}) collective-permute-start(f32[4,1,64,128]{3,2,1,0:T(8,128)S(1)} %get-tuple-element.17), channel_id=1, source_target_pairs={{1,0},{2,1},{3,2},{5,4},{6,5},{7,6},{9,8},{10,9},{11,10},{13,12},{... | collective-permute-start | bytes 393224 | tf_op jit(solution)/shard_map/ppermute | solution.py:20
  69.3 9.0 %collective-permute-start.7 = (f32[4,1,64,128]{3,2,1,0:T(8,128)S(1)}, f32[4,1,64,128]{3,2,1,0:T(8,128)S(1)}, u32[]{:S(2)}, u32[]{:S(2)}) collective-permute-start(f32[4,1,64,128]{3,2,1,0:T(8,128)S(1)} %get-tuple-element.18), channel_id=1, source_target_pairs={{0,1},{1,2},{2,3},{4,5},{5,6},{6,7},{8,9},{9,10},{10,11},{12,13},{... | collective-permute-start | bytes 393224 | tf_op jit(solution)/shard_map/ppermute | solution.py:17
  87.2 69.8 %copy-start.2 = (f32[2,16,64,128]{3,2,1,0:T(8,128)S(1)}, f32[2,16,64,128]{3,2,1,0:T(8,128)}, u32[]{:S(2)}) copy-start(f32[2,16,64,128]{3,2,1,0:T(8,128)} %param.8) | copy-start | bytes 3145732
Sparse Core Ops, SparseCore 0:
  87.3 54.8 all-reduce.5
where the time goes:
time: 167 us; the launch traced here: 166 us
  waiting for transfers between devices  57.8 us (35%)
  blocking collectives  25.2 us (15%)
  starting transfers between devices  24.6 us (15%)
  other arithmetic  24.6 us (15%)
  matrix products  17.1 us (10%)
  between operations  15.6 us (9%)
    psum x1, waiting for transfers between devices, body(): whole = lax.psum(density, 'cls')  55 us
    ppermute x4, starting transfers between devices, padded_2(): lax.ppermute(lax.slice_in_dim(block, block.shape[dim] - width, None, axis...  19.4 us
    dot_general x4, matrix products, body(): jnp.einsum('ct,czxy->tzxy', factor, products[step], precision=lax.Precisi...  17.1 us
    psum x1, blocking collectives, body(): partition = lax.psum(local_part, 'slab') / cells  13 us
    psum x1, blocking collectives, body(): level = lax.psum(jnp.sum(whole[0] + whole[1]), 'slab') / cells  12.1 us
    mul x3, other arithmetic, body(): products.append(forward * q_back[:, step].astype(jnp.float32))  5.55 us
    ppermute x4, starting transfers between devices, padded_2(): lax.ppermute(lax.slice_in_dim(block, 0, width, axis=dim), axis, backward)  5.17 us
    reduce_sum x1, other arithmetic, body(): local_part = jnp.sum(products[0], axis=(1, 2, 3))  4.41 us
  transfers between devices with their start and end apart: 9, of which 3 were waited for; matrix products, arithmetic and copies ran while one was open for 8% of the time, Pallas kernels for 0%

commit v1 on v0

v1 whole, which is shorter than its diff:
```python
import functools
import jax
import jax.numpy as jnp
from jax import lax
from jax.experimental import pallas as pl
from jax.experimental.pallas import tpu as pltpu
from jax.sharding import PartitionSpec as P

flory_chi = 2.0
stiffness = 1.0
mixing = 0.5
diffusion_scale = 0.125
MESH = pl.DeviceIdType.MESH
PAD = 8


def kernel(
    n_cls, n_slab, lanes,
    lengths, steps_count, block_types, q_init_hbm, q_back_hbm, fields_hbm,
    fields_out, q_out,
    q_init, q_back, fields, half, weighted, halo, product, sum_first, sum_all, weight,
    part_slots, level_send, level_recv, level_slots, dens, received, full,
    load_sem, back_sem, halo_send, halo_recv, part_send, part_recv,
    reduce_send, reduce_recv, tile_send, tile_recv, level_ssem, level_rsem, gather_send, gather_recv,
):
    classes, depth, planes, nx, ny = q_back.shape
    me = lax.axis_index("cls")
    slab = lax.axis_index("slab")
    bits = n_cls.bit_length() - 1
    first = me * classes
    cells = float(n_slab * planes * nx * ny)
    groups = nx // 8
    rows = pl.ds(PAD, nx)

    loads = [
        pltpu.make_async_copy(fields_hbm, fields, load_sem.at[0]),
        pltpu.make_async_copy(q_init_hbm, q_init, load_sem.at[1]),
    ]
    back_loads = [
        pltpu.make_async_copy(q_back_hbm.at[:, s], q_back.at[:, s], back_sem.at[s]) for s in range(depth)
    ]
    for copy in loads + back_loads:
        copy.start()

    partners = [me + (1 - 2 * ((me // 2**b) % 2)) * 2**b for b in range(bits)]
    barrier = pltpu.get_barrier_semaphore()
    for partner in partners:
        pl.semaphore_signal(barrier, inc=1, device_id=(partner, slab), device_id_type=MESH)
    for shift in range(1, n_slab):
        pl.semaphore_signal(barrier, inc=1, device_id=(me, (slab + shift) % n_slab), device_id_type=MESH)

    def tile(value):
        return jnp.full((8, ny), value, jnp.float32)

    def step_of(c):
        return tile(lengths[first + c].astype(jnp.float32)) / tile(steps_count[first + c].astype(jnp.float32))

    def as_tiles(value):
        return value.reshape(groups, 8, ny)

    zero_rows = jnp.zeros((PAD, ny), jnp.float32)

    def clear(i, carry):
        for s in range(depth):
            for c in range(classes):
                weighted[s, c, i, pl.ds(0, PAD), :] = zero_rows
                weighted[s, c, i, pl.ds(PAD + nx, PAD), :] = zero_rows
        return carry

    lax.fori_loop(0, planes, clear, 0)

    has_low = slab > 0
    has_high = slab < n_slab - 1

    @pl.when(slab == 0)
    def _():
        halo[:, :, 0] = jnp.zeros((depth, classes, nx, ny), jnp.float32)

    @pl.when(slab == n_slab - 1)
    def _():
        halo[:, :, 1] = jnp.zeros((depth, classes, nx, ny), jnp.float32)

    def to_low(s, c):
        return pltpu.make_async_remote_copy(
            src_ref=weighted.at[s, c, 0, rows], dst_ref=halo.at[s, c, 1],
            send_sem=halo_send.at[s, c, 0], recv_sem=halo_recv.at[s, c, 1],
            device_id=(me, (slab + n_slab - 1) % n_slab), device_id_type=MESH)

    def to_high(s, c):
        return pltpu.make_async_remote_copy(
            src_ref=weighted.at[s, c, planes - 1, rows], dst_ref=halo.at[s, c, 0],
            send_sem=halo_send.at[s, c, 1], recv_sem=halo_recv.at[s, c, 0],
            device_id=(me, (slab + 1) % n_slab), device_id_type=MESH)

    def send_halo(s, c):
        pl.when(has_low)(lambda: to_low(s, c).start())
        pl.when(has_high)(lambda: to_high(s, c).start())

    def prepare(c, z, rate):
        for t in range(2):
            half[c, t, z] = jnp.exp(rate * as_tiles(fields[t, z])).reshape(nx, ny)
        weighted[0, c, z, rows, :] = half[c, block_types[first + c, 0], z] * q_init[c, z].astype(jnp.float32)

    for copy in loads:
        copy.wait()

    def prepare_edges(c, carry):
        rate = (-0.5 * step_of(c))[None]
        prepare(c, 0, rate)
        prepare(c, planes - 1, rate)
        return carry

    lax.fori_loop(0, classes, prepare_edges, 0)
    pl.semaphore_wait(barrier, bits + n_slab - 1)

    def send_first(c, carry):
        send_halo(0, c)
        return carry

    lax.fori_loop(0, classes, send_first, 0)

    def prepare_rest(c, carry):
        rate = (-0.5 * step_of(c))[None]

        def inner(z, carry):
            prepare(c, z, rate)
            return carry

        return lax.fori_loop(1, planes - 1, inner, carry)

    lax.fori_loop(0, classes, prepare_rest, 0)

    column = lax.broadcasted_iota(jnp.int32, (nx, ny), 1)
    at_start = column == 0
    at_end = column == ny - 1

    def part_copy(peer):
        return pltpu.make_async_remote_copy(
            src_ref=sum_first, dst_ref=part_slots.at[slab], send_sem=part_send.at[peer],
            recv_sem=part_recv.at[slab], device_id=(me, peer), device_id_type=MESH)

    def part_wait(peer):
        return pltpu.make_async_remote_copy(
            src_ref=sum_first, dst_ref=part_slots.at[peer], send_sem=part_send.at[peer],
            recv_sem=part_recv.at[peer], device_id=(me, peer), device_id_type=MESH)

    for s in range(depth):
        back_loads[s].wait()

        def advance(c, carry, s=s):
            spread = diffusion_scale * step_of(c)
            keep = (1.0 - 6.0 * spread)[None]
            spread = spread[None]
            kind = block_types[first + c, s]

            def plane(z, below, above, total_sum):
                center = weighted[s, c, z, rows, :]
                total = below + above
                total = total + weighted[s, c, z, pl.ds(PAD - 1, nx), :]
                total = total + weighted[s, c, z, pl.ds(PAD + 1, nx), :]
                total = total + jnp.where(at_start, 0.0, pltpu.roll(center, 1, 1))
                total = total + jnp.where(at_end, 0.0, pltpu.roll(center, ny - 1, 1))
                mixed = keep * as_tiles(center) + spread * as_tiles(total)
                forward = half[c, kind, z] * mixed.reshape(nx, ny)
                value = forward * q_back[c, s, z].astype(jnp.float32)
                product[c, s, z] = value
                if s < depth - 1:
                    weighted[s + 1, c, z, rows, :] = half[c, block_types[first + c, s + 1], z] * forward
                else:
                    q_out[c, z] = forward.astype(jnp.bfloat16)
                return total_sum + jnp.sum(as_tiles(value), axis=0)

            pl.when(has_low)(lambda: to_high(s, c).wait_recv())
            pl.when(has_high)(lambda: to_low(s, c).wait_recv())
            local = jnp.zeros((8, ny), jnp.float32)
            local = plane(0, halo[s, c, 0], weighted[s, c, 1, rows, :], local)
            local = plane(planes - 1, weighted[s, c, planes - 2, rows, :], halo[s, c, 1], local)
            if s < depth - 1:
                send_halo(s + 1, c)
            local = lax.fori_loop(
                1, planes - 1,
                lambda z, acc: plane(z, weighted[s, c, z - 1, rows, :], weighted[s, c, z + 1, rows, :], acc),
                local)
            if s == 0:
                sum_first[c] = local
                sum_all[c] = local
            else:
                sum_all[c] = sum_all[c] + local
            return carry

        lax.fori_loop(0, classes, advance, 0)
        if s == 0:
            for shift in range(1, n_slab):
                part_copy((slab + shift) % n_slab).start()

    for shift in range(1, n_slab):
        part_wait((slab + shift) % n_slab).wait_recv()
    part_slots[slab] = sum_first[...]
    length_sum = lengths[0]
    for i in range(1, lengths.shape[0]):
        length_sum = length_sum + lengths[i]
    length_sum = tile(length_sum.astype(jnp.float32))
    level = jnp.zeros((8, ny), jnp.float32)
    for c in range(classes):
        whole = part_slots[0, c]
        for i in range(1, n_slab):
            whole = whole + part_slots[i, c]
        partition = tile(jnp.sum(whole)) / cells
        fraction = tile(lengths[first + c].astype(jnp.float32)) / length_sum
        scale = fraction * step_of(c) / partition
        level = level + scale * sum_all[c]
        for s in range(depth):
            second = scale * block_types[first + c, s].astype(jnp.float32)
            weight[c, s, 0] = scale - second
            weight[c, s, 1] = second

    lane_rows = dens.shape[0] // lanes
    lane_planes = planes // lanes
    orders = []
    for lane in range(lanes):
        tail = list(range(1, bits))
        orders.append(([0] if bits else []) + (tail if lane % 2 == 0 else tail[::-1]))

    def flip(b):
        return (me // 2**b) % 2

    def window(lane, phase):
        start, size = lane * lane_rows, lane_rows
        for j in range(phase):
            size = size // 2
            start = start + flip(orders[lane][j]) * size
        return start, size

    def at(start, size):
        return pl.ds(pl.multiple_of(start, 8), size)

    def reduce_copy(lane, phase):
        start, size = window(lane, phase)
        b = orders[lane][phase]
        size = size // 2
        into = lane * lane_rows + lane_rows - lane_rows // 2**phase
        return pltpu.make_async_remote_copy(
            src_ref=dens.at[at(start + (1 - flip(b)) * size, size)], dst_ref=received.at[pl.ds(into, size)],
            send_sem=reduce_send.at[lane, phase], recv_sem=reduce_recv.at[lane, phase],
            device_id=(partners[b], slab), device_id_type=MESH)

    def tile_copy(phase):
        return pltpu.make_async_remote_copy(
            src_ref=level_send.at[phase], dst_ref=level_recv.at[phase],
            send_sem=tile_send.at[phase], recv_sem=tile_recv.at[phase],
            device_id=(partners[phase], slab), device_id_type=MESH)

    def gather_copy(lane, phase):
        start, size = window(lane, phase + 1)
        b = orders[lane][phase]
        return pltpu.make_async_remote_copy(
            src_ref=full.at[at(start, size)], dst_ref=full.at[at(start, size)],
            send_sem=gather_send.at[lane, phase], recv_sem=gather_recv.at[lane, phase],
            device_id=(partners[b], slab), device_id_type=MESH)

    def gather_wait(lane, phase):
        start, size = window(lane, phase)
        b = orders[lane][phase]
        size = size // 2
        there = at(start + (1 - flip(b)) * size, size)
        return pltpu.make_async_remote_copy(
            src_ref=full.at[there], dst_ref=full.at[there],
            send_sem=gather_send.at[lane, phase], recv_sem=gather_recv.at[lane, phase],
            device_id=(partners[b], slab), device_id_type=MESH)

    def level_copy(peer):
        return pltpu.make_async_remote_copy(
            src_ref=level_send.at[bits], dst_ref=level_slots.at[slab], send_sem=level_ssem.at[peer],
            recv_sem=level_rsem.at[slab], device_id=(me, peer), device_id_type=MESH)

    def level_wait(peer):
        return pltpu.make_async_remote_copy(
            src_ref=level_send.at[bits], dst_ref=level_slots.at[peer], send_sem=level_ssem.at[peer],
            recv_sem=level_rsem.at[peer], device_id=(me, peer), device_id_type=MESH)

    level_send[0] = level
    if bits:
        tile_copy(0).start()

    for lane in range(lanes):
        def combine(z, carry):
            one = jnp.zeros((groups, 8, ny), jnp.float32)
            two = one
            for c in range(classes):
                for s in range(depth):
                    value = as_tiles(product[c, s, z])
                    one = one + weight[c, s, 0][None] * value
                    two = two + weight[c, s, 1][None] * value
            dens[at(z * 2 * nx, nx)] = one.reshape(nx, ny)
            dens[at(z * 2 * nx + nx, nx)] = two.reshape(nx, ny)
            return carry

        lax.fori_loop(lane * lane_planes, (lane + 1) * lane_planes, combine, 0)
        if bits:
            reduce_copy(lane, 0).start()

    for phase in range(bits):
        tile_copy(phase).wait_recv()
        level_send[phase + 1] = level_send[phase] + level_recv[phase]
        if phase < bits - 1:
            tile_copy(phase + 1).start()
        else:
            for shift in range(1, n_slab):
                level_copy((slab + shift) % n_slab).start()
        for lane in range(lanes):
            reduce_copy(lane, phase).wait_recv()
            start, size = window(lane, phase + 1)
            into = lane * lane_rows + lane_rows - lane_rows // 2**phase
            value = dens[at(start, size)] + received[pl.ds(into, size)]
            if phase < bits - 1:
                dens[at(start, size)] = value
                reduce_copy(lane, phase + 1).start()
            else:
                full[at(start, size)] = value
                gather_copy(lane, phase).start()
    for phase in reversed(range(bits)):
        for lane in range(lanes):
            gather_wait(lane, phase).wait_recv()
            if phase > 0:
                gather_copy(lane, phase - 1).start()

    for shift in range(1, n_slab):
        level_wait((slab + shift) % n_slab).wait_recv()
    level_slots[slab] = level_send[bits]
    level = level_slots[0]
    for i in range(1, n_slab):
        level = level + level_slots[i]
    level = (tile(jnp.sum(level)) / cells)[None]

    def finish(z, carry):
        one = as_tiles(full[at(z * 2 * nx, nx)])
        two = as_tiles(full[at(z * 2 * nx + nx, nx)])
        pressure = stiffness * (one + two - level)
        for t, other in ((0, two), (1, one)):
            old = as_tiles(fields[t, z])
            fields_out[t, z] = (old + mixing * (flory_chi * other + pressure - old)).reshape(nx, ny)
        return carry

    lax.fori_loop(0, planes, finish, 0)

    for s in range(depth):
        def drain(c, carry, s=s):
            pl.when(has_low)(lambda: to_low(s, c).wait_send())
            pl.when(has_high)(lambda: to_high(s, c).wait_send())
            return carry

        lax.fori_loop(0, classes, drain, 0)
    for shift in range(1, n_slab):
        part_copy((slab + shift) % n_slab).wait_send()
        level_copy((slab + shift) % n_slab).wait_send()
    for phase in range(bits):
        tile_copy(phase).wait_send()
        for lane in range(lanes):
            reduce_copy(lane, phase).wait_send()
            gather_copy(lane, phase).wait_send()


def body(n_cls, n_slab, q_init, q_back, fields, lengths, steps_count, block_types):
    classes, depth, planes, nx, ny = q_back.shape
    lanes = 4
    bits = n_cls.bit_length() - 1
    assert n_cls == 2**bits and n_slab > 1 and planes % lanes == 0
    rows = planes * 2 * nx
    f32, bf16 = jnp.float32, jnp.bfloat16
    dma = pltpu.SemaphoreType.DMA
    smem = pl.BlockSpec(memory_space=pltpu.SMEM)
    vmem = pl.BlockSpec(memory_space=pltpu.VMEM)
    hbm = pl.BlockSpec(memory_space=pl.ANY)
    return pl.pallas_call(
        functools.partial(kernel, n_cls, n_slab, lanes),
        out_shape=(
            jax.ShapeDtypeStruct(fields.shape, f32),
            jax.ShapeDtypeStruct(q_init.shape, bf16),
        ),
        in_specs=[smem, smem, smem, hbm, hbm, hbm],
        out_specs=(vmem, vmem),
        scratch_shapes=[
            pltpu.VMEM(q_init.shape, bf16),
            pltpu.VMEM(q_back.shape, bf16),
            pltpu.VMEM(fields.shape, f32),
            pltpu.VMEM((classes, 2, planes, nx, ny), f32),
            pltpu.VMEM((depth, classes, planes, nx + 2 * PAD, ny), f32),
            pltpu.VMEM((depth, classes, 2, nx, ny), f32),
            pltpu.VMEM((classes, depth, planes, nx, ny), f32),
            pltpu.VMEM((classes, 8, ny), f32),
            pltpu.VMEM((classes, 8, ny), f32),
            pltpu.VMEM((classes, depth, 2, 8, ny), f32),
            pltpu.VMEM((n_slab, classes, 8, ny), f32),
            pltpu.VMEM((bits + 1, 8, ny), f32),
            pltpu.VMEM((max(bits, 1), 8, ny), f32),
            pltpu.VMEM((n_slab, 8, ny), f32),
            pltpu.VMEM((rows, ny), f32),
            pltpu.VMEM((rows, ny), f32),
            pltpu.VMEM((rows, ny), f32),
            dma((2,)),
            dma((depth,)),
            dma((depth, classes, 2)),
            dma((depth, classes, 2)),
            dma((n_slab,)),
            dma((n_slab,)),
            dma((lanes, bits)),
            dma((lanes, bits)),
            dma((bits,)),
            dma((bits,)),
            dma((n_slab,)),
            dma((n_slab,)),
            dma((lanes, bits)),
            dma((lanes, bits)),
        ],
        compiler_params=pltpu.CompilerParams(
            collective_id=0, has_side_effects=True, vmem_limit_bytes=52 * 1024 * 1024
        ),
        cost_estimate=pl.CostEstimate(
            flops=20 * q_back.size, bytes_accessed=8 * 1024 * 1024, transcendentals=2 * q_init.size
        ),
    )(lengths, steps_count, block_types, q_init, q_back, fields)


def solution(mesh):
    return jax.shard_map(
        functools.partial(body, mesh.shape["cls"], mesh.shape["slab"]),
        mesh=mesh,
        in_specs=(
            P("cls", "slab", None, None),
            P("cls", None, "slab", None, None),
            P(None, "slab", None, None),
            P(),
            P(),
            P(),
        ),
        out_specs=(P(None, "slab", None, None), P("cls", "slab", None, None)),
        check_vma=False,
    )
```

time: 167 us -> 59.2 us (0.35)
  waiting for transfers between devices: 57.8 us -> 0 us
  Pallas kernels: 0 us -> 52.6 us
  blocking collectives: 25.2 us -> 0 us
  other arithmetic: 24.6 us -> 0 us
  starting transfers between devices: 24.6 us -> 0 us
  matrix products: 17.1 us -> 0 us
  between operations: 15.6 us -> 0.64 us
  local copies, waits for them, and re-layouts: 1.48 us -> 5.31 us
    psum x1 -> x0, waiting for transfers between devices: 55 us -> none  [body(): whole = lax.psum(density, 'cls')]
    pallas_call x0 -> x1, Pallas kernels: none -> 52.6 us  [body(): pl.pallas_call(functools.partial(kernel, n_cls, n_slab, lanes), out_shape...]
    psum x2 -> x0, blocking collectives: 25.2 us -> none  [the longest x1 13 us: body(): partition = lax.psum(local_part, 'slab') / cells]
    ppermute x8 -> x0, starting transfers between devices: 24.6 us -> none  [the longest x4 19.4 us: padded_2(): lax.ppermute(lax.slice_in_dim(block, block.shape[dim] - width, None, axis...]
    dot_general x4 -> x0, matrix products: 17.1 us -> none  [body(): jnp.einsum('ct,czxy->tzxy', factor, products[step], precision=lax.Precisi...]
    mul x8 -> x0, other arithmetic: 9.26 us -> none  [the longest x3 5.55 us: body(): products.append(forward * q_back[:, step].astype(jnp.float32))]
    reduce_sum x3 -> x0, other arithmetic: 7.72 us -> none  [the longest x1 4.41 us: body(): local_part = jnp.sum(products[0], axis=(1, 2, 3))]
    unnamed x8 -> x7, local copies, waits for them, and re-layouts: 0.02 us -> 5.31 us
  transfers between devices with their start and end apart: 9 -> 0, of which waited for: 3 -> 0; matrix products, arithmetic and copies ran while one was open for 8% -> 0% of each run, Pallas kernels for 0% -> 0%
where the time goes in v1:
time: 59.2 us; the launch traced here: 58.5 us
  Pallas kernels  52.6 us (89%)
  local copies, waits for them, and re-layouts  5.31 us (9%)
  between operations  0.64 us (1%)
    pallas_call x1, Pallas kernels, body(): pl.pallas_call(functools.partial(kernel, n_cls, n_slab, lanes), out_shape...  52.6 us
    unnamed x7, local copies, waits for them, and re-layouts  5.31 us

profile of v1, /device:TPU:0, one launch (start us, length us, event | category | flops | bytes accessed | tf_op | source)
XLA Modules:
  0.0 58.5 jit_solution(2220522937685969225)
XLA Ops:
  0.6 0.8 %copy.8.block_types = s32[32,4]{1,0:T(8,128)S(1)} copy(s32[32,4]{0,1:T(4,128)} %param.11) | data formatting | bytes 1024 | tf_op args[5]
  1.4 0.0 copy-start
  1.4 0.7 %copy-done = s32[32]{0:T(128)S(1)} copy-done((s32[32]{0:T(128)S(1)}, s32[32]{0:T(128)}, u32[]{:S(2)}) %copy-start) | copy-done | bytes 152
  2.0 0.0 copy-start.1
  2.1 0.7 %copy-done.1 = s32[32]{0:T(128)S(1)} copy-done((s32[32]{0:T(128)S(1)}, s32[32]{0:T(128)}, u32[]{:S(2)}) %copy-start.1) | copy-done | bytes 152
  2.7 52.6 %shard_map.77 = (f32[2,16,64,128]{3,2,1,0:T(8,128)S(1)}, bf16[4,16,64,128]{3,2,1,0:T(8,128)(2,1)}) custom-call(s32[32]{0:T(128)S(1)} %copy-done, s32[32]{0:T(128)S(1)} %copy-done.1, s32[32,4]{1,0:T(8,128)S(1)} %copy.8.block_types, bf16[4,16,64,128]{3,2,1,0:T(8,128)(2,1)} %q_init_hbm.1, bf16[4,4,16,64,128]{4,3,2,1,0:T(8,128)(2,1)} %q_back_hbm.1, ...), custom_call_target="tpu_custom_call" | custom-call | flops 41943040 | bytes 8388608 | tf_op jit(solution)/shard_map/pallas_call | solution.py:374
  55.3 1.0 %copy.11 = f32[2,16,64,128]{3,2,1,0:T(8,128)} copy(f32[2,16,64,128]{3,2,1,0:T(8,128)S(1)} %get-tuple-element.4) | data formatting | bytes 2097152
  56.3 2.3 %copy.12 = bf16[4,16,64,128]{3,2,1,0:T(8,128)(2,1)} copy(bf16[4,16,64,128]{3,2,1,0:T(8,128)(2,1)} %get-tuple-element.5) | data formatting | bytes 2097152
Async XLA Ops:
  1.4 0.7 %copy-start = (s32[32]{0:T(128)S(1)}, s32[32]{0:T(128)}, u32[]{:S(2)}) copy-start(s32[32]{0:T(128)} %lengths.1) | copy-start | bytes 388
  2.0 0.7 %copy-start.1 = (s32[32]{0:T(128)S(1)}, s32[32]{0:T(128)}, u32[]{:S(2)}) copy-start(s32[32]{0:T(128)} %steps_count.1) | copy-start | bytes 388

commit v2 on v1

--- a/solution.py
+++ b/solution.py
@@ -16,7 +16,7 @@
 
 def kernel(
     n_cls, n_slab, lanes,
-    lengths, steps_count, block_types, q_init_hbm, q_back_hbm, fields_hbm,
+    numbers, q_init_hbm, q_back_hbm, fields_hbm,
     fields_out, q_out,
     q_init, q_back, fields, half, weighted, halo, product, sum_first, sum_all, weight,
     part_slots, level_send, level_recv, level_slots, dens, received, full,
@@ -24,6 +24,17 @@
     reduce_send, reduce_recv, tile_send, tile_recv, level_ssem, level_rsem, gather_send, gather_recv,
 ):
     classes, depth, planes, nx, ny = q_back.shape
+    everyone = n_cls * classes
+
+    def length_of(c):
+        return numbers[c].astype(jnp.float32)
+
+    def count_of(c):
+        return numbers[everyone + c].astype(jnp.float32)
+
+    def kind_of(c, s):
+        return numbers[2 * everyone + s * everyone + first + c]
+
     me = lax.axis_index("cls")
     slab = lax.axis_index("slab")
     bits = n_cls.bit_length() - 1
@@ -31,6 +42,7 @@
     cells = float(n_slab * planes * nx * ny)
     groups = nx // 8
     rows = pl.ds(PAD, nx)
+    block = max(k for k in range(1, 8) if (planes - 2) % k == 0)
 
     loads = [
         pltpu.make_async_copy(fields_hbm, fields, load_sem.at[0]),
@@ -53,7 +65,7 @@
         return jnp.full((8, ny), value, jnp.float32)
 
     def step_of(c):
-        return tile(lengths[first + c].astype(jnp.float32)) / tile(steps_count[first + c].astype(jnp.float32))
+        return tile(length_of(first + c)) / tile(count_of(first + c))
 
     def as_tiles(value):
         return value.reshape(groups, 8, ny)
@@ -63,8 +75,8 @@
     def clear(i, carry):
         for s in range(depth):
             for c in range(classes):
-                weighted[s, c, i, pl.ds(0, PAD), :] = zero_rows
-                weighted[s, c, i, pl.ds(PAD + nx, PAD), :] = zero_rows
+                weighted[s][c, i, pl.ds(0, PAD), :] = zero_rows
+                weighted[s][c, i, pl.ds(PAD + nx, PAD), :] = zero_rows
         return carry
 
     lax.fori_loop(0, planes, clear, 0)
@@ -82,13 +94,13 @@
 
     def to_low(s, c):
         return pltpu.make_async_remote_copy(
-            src_ref=weighted.at[s, c, 0, rows], dst_ref=halo.at[s, c, 1],
+            src_ref=weighted[s].at[c, 0, rows], dst_ref=halo.at[s, c, 1],
             send_sem=halo_send.at[s, c, 0], recv_sem=halo_recv.at[s, c, 1],
             device_id=(me, (slab + n_slab - 1) % n_slab), device_id_type=MESH)
 
     def to_high(s, c):
         return pltpu.make_async_remote_copy(
-            src_ref=weighted.at[s, c, planes - 1, rows], dst_ref=halo.at[s, c, 0],
+            src_ref=weighted[s].at[c, planes - 1, rows], dst_ref=halo.at[s, c, 0],
             send_sem=halo_send.at[s, c, 1], recv_sem=halo_recv.at[s, c, 0],
             device_id=(me, (slab + 1) % n_slab), device_id_type=MESH)
 
@@ -96,18 +108,20 @@
         pl.when(has_low)(lambda: to_low(s, c).start())
         pl.when(has_high)(lambda: to_high(s, c).start())
 
-    def prepare(c, z, rate):
-        for t in range(2):
-            half[c, t, z] = jnp.exp(rate * as_tiles(fields[t, z])).reshape(nx, ny)
-        weighted[0, c, z, rows, :] = half[c, block_types[first + c, 0], z] * q_init[c, z].astype(jnp.float32)
+    def prepare(c, where, rate):
+        for z in where:
+            values = [jnp.exp(rate * as_tiles(fields[t, z])).reshape(nx, ny) for t in range(2)]
+            start = q_init[c, z].astype(jnp.float32)
+            for t in range(2):
+                half[c, t, z] = values[t]
+            weighted[0][c, z, rows, :] = jnp.where(kind_of(c, 0) == 0, values[0], values[1]) * start
 
     for copy in loads:
         copy.wait()
 
     def prepare_edges(c, carry):
         rate = (-0.5 * step_of(c))[None]
-        prepare(c, 0, rate)
-        prepare(c, planes - 1, rate)
+        prepare(c, (0, planes - 1), rate)
         return carry
 
     lax.fori_loop(0, classes, prepare_edges, 0)
@@ -122,17 +136,17 @@
     def prepare_rest(c, carry):
         rate = (-0.5 * step_of(c))[None]
 
-        def inner(z, carry):
-            prepare(c, z, rate)
+        def inner(i, carry):
+            prepare(c, [1 + i * block + k for k in range(block)], rate)
             return carry
 
-        return lax.fori_loop(1, planes - 1, inner, carry)
+        return lax.fori_loop(0, (planes - 2) // block, inner, carry)
 
     lax.fori_loop(0, classes, prepare_rest, 0)
 
-    column = lax.broadcasted_iota(jnp.int32, (nx, ny), 1)
-    at_start = column == 0
-    at_end = column == ny - 1
+    column = lax.broadcasted_iota(jnp.int32, (8, ny), 1)
+    not_start = jnp.where(column == 0, 0.0, 1.0)[None]
+    not_end = jnp.where(column == ny - 1, 0.0, 1.0)[None]
 
     def part_copy(peer):
         return pltpu.make_async_remote_copy(
@@ -151,36 +165,52 @@
             spread = diffusion_scale * step_of(c)
             keep = (1.0 - 6.0 * spread)[None]
             spread = spread[None]
-            kind = block_types[first + c, s]
-
-            def plane(z, below, above, total_sum):
-                center = weighted[s, c, z, rows, :]
+            kind = kind_of(c, s)
+            now = weighted[s]
+
+            def spreads(z, below, center, above):
                 total = below + above
-                total = total + weighted[s, c, z, pl.ds(PAD - 1, nx), :]
-                total = total + weighted[s, c, z, pl.ds(PAD + 1, nx), :]
-                total = total + jnp.where(at_start, 0.0, pltpu.roll(center, 1, 1))
-                total = total + jnp.where(at_end, 0.0, pltpu.roll(center, ny - 1, 1))
-                mixed = keep * as_tiles(center) + spread * as_tiles(total)
-                forward = half[c, kind, z] * mixed.reshape(nx, ny)
+                total = total + now[c, z, pl.ds(PAD - 1, nx), :]
+                total = total + now[c, z, pl.ds(PAD + 1, nx), :]
+                total = as_tiles(total) + not_start * as_tiles(pltpu.roll(center, 1, 1))
+                total = total + not_end * as_tiles(pltpu.roll(center, ny - 1, 1))
+                return (keep * as_tiles(center) + spread * total).reshape(nx, ny)
+
+            def finish_plane(z, mixed):
+                forward = half[c, kind, z] * mixed
                 value = forward * q_back[c, s, z].astype(jnp.float32)
-                product[c, s, z] = value
                 if s < depth - 1:
-                    weighted[s + 1, c, z, rows, :] = half[c, block_types[first + c, s + 1], z] * forward
+                    ahead = half[c, kind_of(c, s + 1), z]
+                    weighted[s + 1][c, z, rows, :] = ahead * forward
                 else:
                     q_out[c, z] = forward.astype(jnp.bfloat16)
-                return total_sum + jnp.sum(as_tiles(value), axis=0)
+                product[s][c, z] = value
+                return jnp.sum(as_tiles(value), axis=0)
 
             pl.when(has_low)(lambda: to_high(s, c).wait_recv())
             pl.when(has_high)(lambda: to_low(s, c).wait_recv())
-            local = jnp.zeros((8, ny), jnp.float32)
-            local = plane(0, halo[s, c, 0], weighted[s, c, 1, rows, :], local)
-            local = plane(planes - 1, weighted[s, c, planes - 2, rows, :], halo[s, c, 1], local)
+            last = planes - 1
+            bottom = spreads(0, halo[s, c, 0], now[c, 0, rows, :], now[c, 1, rows, :])
+            top = spreads(last, now[c, last - 1, rows, :], now[c, last, rows, :], halo[s, c, 1])
+            local = finish_plane(0, bottom) + finish_plane(last, top)
             if s < depth - 1:
                 send_halo(s + 1, c)
-            local = lax.fori_loop(
-                1, planes - 1,
-                lambda z, acc: plane(z, weighted[s, c, z - 1, rows, :], weighted[s, c, z + 1, rows, :], acc),
-                local)
+
+            def inner(i, total_sum):
+                base = 1 + i * block
+                below = now[c, base - 1, rows, :]
+                center = now[c, base, rows, :]
+                waiting = None
+                for k in range(block):
+                    above = now[c, base + k + 1, rows, :]
+                    mixed = spreads(base + k, below, center, above)
+                    below, center = center, above
+                    if k:
+                        total_sum = total_sum + finish_plane(base + k - 1, waiting)
+                    waiting = mixed
+                return total_sum + finish_plane(base + block - 1, waiting)
+
+            local = lax.fori_loop(0, (planes - 2) // block, inner, local)
             if s == 0:
                 sum_first[c] = local
                 sum_all[c] = local
@@ -196,9 +226,9 @@
     for shift in range(1, n_slab):
         part_wait((slab + shift) % n_slab).wait_recv()
     part_slots[slab] = sum_first[...]
-    length_sum = lengths[0]
-    for i in range(1, lengths.shape[0]):
-        length_sum = length_sum + lengths[i]
+    length_sum = numbers[0]
+    for i in range(1, everyone):
+        length_sum = length_sum + numbers[i]
     length_sum = tile(length_sum.astype(jnp.float32))
     level = jnp.zeros((8, ny), jnp.float32)
     for c in range(classes):
@@ -206,11 +236,11 @@
         for i in range(1, n_slab):
             whole = whole + part_slots[i, c]
         partition = tile(jnp.sum(whole)) / cells
-        fraction = tile(lengths[first + c].astype(jnp.float32)) / length_sum
+        fraction = tile(length_of(first + c)) / length_sum
         scale = fraction * step_of(c) / partition
         level = level + scale * sum_all[c]
         for s in range(depth):
-            second = scale * block_types[first + c, s].astype(jnp.float32)
+            second = scale * kind_of(c, s).astype(jnp.float32)
             weight[c, s, 0] = scale - second
             weight[c, s, 1] = second
 
@@ -288,7 +318,7 @@
             two = one
             for c in range(classes):
                 for s in range(depth):
-                    value = as_tiles(product[c, s, z])
+                    value = as_tiles(product[s][c, z])
                     one = one + weight[c, s, 0][None] * value
                     two = two + weight[c, s, 1][None] * value
             dens[at(z * 2 * nx, nx)] = one.reshape(nx, ny)
@@ -366,27 +396,28 @@
     bits = n_cls.bit_length() - 1
     assert n_cls == 2**bits and n_slab > 1 and planes % lanes == 0
     rows = planes * 2 * nx
+    numbers = jnp.concatenate([lengths, steps_count, block_types.T.reshape(-1)])
     f32, bf16 = jnp.float32, jnp.bfloat16
     dma = pltpu.SemaphoreType.DMA
     smem = pl.BlockSpec(memory_space=pltpu.SMEM)
     vmem = pl.BlockSpec(memory_space=pltpu.VMEM)
-    hbm = pl.BlockSpec(memory_space=pl.ANY)
+    hbm = pl.BlockSpec(memory_space=pltpu.HBM)
     return pl.pallas_call(
         functools.partial(kernel, n_cls, n_slab, lanes),
         out_shape=(
             jax.ShapeDtypeStruct(fields.shape, f32),
             jax.ShapeDtypeStruct(q_init.shape, bf16),
         ),
-        in_specs=[smem, smem, smem, hbm, hbm, hbm],
+        in_specs=[smem, hbm, hbm, hbm],
         out_specs=(vmem, vmem),
         scratch_shapes=[
             pltpu.VMEM(q_init.shape, bf16),
             pltpu.VMEM(q_back.shape, bf16),
             pltpu.VMEM(fields.shape, f32),
             pltpu.VMEM((classes, 2, planes, nx, ny), f32),
-            pltpu.VMEM((depth, classes, planes, nx + 2 * PAD, ny), f32),
+            [pltpu.VMEM((classes, planes, nx + 2 * PAD, ny), f32)] * depth,
             pltpu.VMEM((depth, classes, 2, nx, ny), f32),
-            pltpu.VMEM((classes, depth, planes, nx, ny), f32),
+            [pltpu.VMEM((classes, planes, nx, ny), f32)] * depth,
             pltpu.VMEM((classes, 8, ny), f32),
             pltpu.VMEM((classes, 8, ny), f32),
             pltpu.VMEM((classes, depth, 2, 8, ny), f32),
@@ -413,12 +444,12 @@
             dma((lanes, bits)),
         ],
         compiler_params=pltpu.CompilerParams(
-            collective_id=0, has_side_effects=True, vmem_limit_bytes=52 * 1024 * 1024
+            collective_id=0, has_side_effects=True, vmem_limit_bytes=51 * 1024 * 1024
         ),
         cost_estimate=pl.CostEstimate(
             flops=20 * q_back.size, bytes_accessed=8 * 1024 * 1024, transcendentals=2 * q_init.size
         ),
-    )(lengths, steps_count, block_types, q_init, q_back, fields)
+    )(numbers, q_init, q_back, fields)
 
 
 def solution(mesh):

time: 59.2 us -> 46.9 us (0.79)
  Pallas kernels: 52.6 us -> 42.1 us
  local copies, waits for them, and re-layouts: 5.31 us -> 2.71 us
  other arithmetic: 0 us -> 0.75 us
    pallas_call x1, Pallas kernels: 52.6 us -> 42.1 us  [body(): pl.pallas_call(functools.partial(kernel, n_cls, n_slab, lanes), out_shape...]
    unnamed x7 -> x2, local copies, waits for them, and re-layouts: 5.31 us -> 1.94 us
    reshape x0 -> x1, local copies, waits for them, and re-layouts: none -> 0.76 us  [body(): numbers = jnp.concatenate([lengths, steps_count, block_types.T.reshape(-1)])]
    concatenate x0 -> x1, other arithmetic: none -> 0.75 us  [body(): numbers = jnp.concatenate([lengths, steps_count, block_types.T.reshape(-1)])]
where the time goes in v2:
time: 46.9 us; the launch traced here: 46.2 us
  Pallas kernels  42.1 us (90%)
  local copies, waits for them, and re-layouts  2.71 us (6%)
  other arithmetic  0.75 us (2%)
  between operations  0.64 us (1%)
    pallas_call x1, Pallas kernels, body(): pl.pallas_call(functools.partial(kernel, n_cls, n_slab, lanes), out_shape...  42.1 us
    unnamed x2, local copies, waits for them, and re-layouts  1.94 us

profile of v2, /device:TPU:0, one launch (start us, length us, event | category | flops | bytes accessed | tf_op | source)
XLA Modules:
  0.0 46.2 jit_solution(4631736663276037028)
XLA Ops:
  0.6 0.8 %reshape.7 = s32[128]{0:T(128)S(1)} reshape(s32[4,32]{1,0:T(4,128)} %bitcast.1) | data formatting | bytes 1024 | tf_op jit(solution)/shard_map/reshape | solution.py:399
  1.4 0.7 %pad_add_fusion.numbers = s32[192]{0:T(256)S(1)} fusion(s32[128]{0:T(128)S(1)} %reshape.7, s32[32]{0:T(128)} %param.10, s32[32]{0:T(128)} %param.9), kind=kLoop, calls=%fused_computation | loop fusion | flops 384 | bytes 1536 | tf_op jit(solution)/shard_map/concatenate | solution.py:399
  2.1 42.1 %shard_map.77 = (f32[2,16,64,128]{3,2,1,0:T(8,128)S(1)}, bf16[4,16,64,128]{3,2,1,0:T(8,128)(2,1)S(1)}) custom-call(s32[192]{0:T(256)S(1)} %pad_add_fusion.numbers, bf16[4,16,64,128]{3,2,1,0:T(8,128)(2,1)} %q_init_hbm.1, bf16[4,4,16,64,128]{4,3,2,1,0:T(8,128)(2,1)} %q_back_hbm.1, f32[2,16,64,128]{3,2,1,0:T(8,128)} %fields_hbm.1), custom_call_target="tpu_custom_call" | custom-call | flops 41943040 | bytes 8388608 | tf_op jit(solution)/shard_map/pallas_call | solution.py:405
  44.3 1.0 %copy.10 = f32[2,16,64,128]{3,2,1,0:T(8,128)} copy(f32[2,16,64,128]{3,2,1,0:T(8,128)S(1)} %get-tuple-element.4) | data formatting | bytes 2097152
  45.2 1.0 %copy.11 = bf16[4,16,64,128]{3,2,1,0:T(8,128)(2,1)} copy(bf16[4,16,64,128]{3,2,1,0:T(8,128)(2,1)S(1)} %get-tuple-element.5) | data formatting | bytes 2097152

commit v3 on v2

--- a/solution.py
+++ b/solution.py
@@ -18,7 +18,7 @@
     n_cls, n_slab, lanes,
     numbers, q_init_hbm, q_back_hbm, fields_hbm,
     fields_out, q_out,
-    q_init, q_back, fields, half, weighted, halo, product, sum_first, sum_all, weight,
+    q_init, q_back, fields, half, weighted, halo, product, sum_first, sum_all, scales, weight,
     part_slots, level_send, level_recv, level_slots, dens, received, full,
     load_sem, back_sem, halo_send, halo_recv, part_send, part_recv,
     reduce_send, reduce_recv, tile_send, tile_recv, level_ssem, level_rsem, gather_send, gather_recv,
@@ -158,91 +158,107 @@
             src_ref=sum_first, dst_ref=part_slots.at[peer], send_sem=part_send.at[peer],
             recv_sem=part_recv.at[peer], device_id=(me, peer), device_id_type=MESH)
 
-    for s in range(depth):
+    def stepper(s, c):
+        spread = diffusion_scale * step_of(c)
+        keep = (1.0 - 6.0 * spread)[None]
+        spread = spread[None]
+        kind = kind_of(c, s)
+        now = weighted[s]
+
+        def spreads(z, below, center, above):
+            total = below + above
+            total = total + now[c, z, pl.ds(PAD - 1, nx), :]
+            total = total + now[c, z, pl.ds(PAD + 1, nx), :]
+            total = as_tiles(total) + not_start * as_tiles(pltpu.roll(center, 1, 1))
+            total = total + not_end * as_tiles(pltpu.roll(center, ny - 1, 1))
+            return (keep * as_tiles(center) + spread * total).reshape(nx, ny)
+
+        def finish_plane(z, mixed):
+            forward = half[c, kind, z] * mixed
+            value = forward * q_back[c, s, z].astype(jnp.float32)
+            if s < depth - 1:
+                ahead = half[c, kind_of(c, s + 1), z]
+                weighted[s + 1][c, z, rows, :] = ahead * forward
+            else:
+                q_out[c, z] = forward.astype(jnp.bfloat16)
+            product[s][c, z] = value
+            return jnp.sum(as_tiles(value), axis=0)
+
+        return spreads, finish_plane
+
+    def run(s, c, base, count, total_sum):
+        spreads, finish_plane = stepper(s, c)
+        now = weighted[s]
+        below = now[c, base - 1, rows, :]
+        center = now[c, base, rows, :]
+        waiting = None
+        for k in range(count):
+            above = now[c, base + k + 1, rows, :]
+            mixed = spreads(base + k, below, center, above)
+            below, center = center, above
+            if k:
+                total_sum = total_sum + finish_plane(base + k - 1, waiting)
+            waiting = mixed
+        return total_sum + finish_plane(base + count - 1, waiting)
+
+    def middle(s):
         back_loads[s].wait()
-
-        def advance(c, carry, s=s):
-            spread = diffusion_scale * step_of(c)
-            keep = (1.0 - 6.0 * spread)[None]
-            spread = spread[None]
-            kind = kind_of(c, s)
+        count = planes - 2 - 2 * s
+        block = max(k for k in range(1, 8) if count % k == 0)
+
+        def each(c, carry):
+            local = lax.fori_loop(
+                0, count // block, lambda i, acc: run(s, c, s + 1 + i * block, block, acc),
+                jnp.zeros((8, ny), jnp.float32))
+            sum_all[c] = local if s == 0 else sum_all[c] + local
+            return carry
+
+        lax.fori_loop(0, classes, each, 0)
+
+    def ends(s):
+        def each(c, carry):
+            spreads, finish_plane = stepper(s, c)
             now = weighted[s]
-
-            def spreads(z, below, center, above):
-                total = below + above
-                total = total + now[c, z, pl.ds(PAD - 1, nx), :]
-                total = total + now[c, z, pl.ds(PAD + 1, nx), :]
-                total = as_tiles(total) + not_start * as_tiles(pltpu.roll(center, 1, 1))
-                total = total + not_end * as_tiles(pltpu.roll(center, ny - 1, 1))
-                return (keep * as_tiles(center) + spread * total).reshape(nx, ny)
-
-            def finish_plane(z, mixed):
-                forward = half[c, kind, z] * mixed
-                value = forward * q_back[c, s, z].astype(jnp.float32)
-                if s < depth - 1:
-                    ahead = half[c, kind_of(c, s + 1), z]
-                    weighted[s + 1][c, z, rows, :] = ahead * forward
-                else:
-                    q_out[c, z] = forward.astype(jnp.bfloat16)
-                product[s][c, z] = value
-                return jnp.sum(as_tiles(value), axis=0)
-
             pl.when(has_low)(lambda: to_high(s, c).wait_recv())
             pl.when(has_high)(lambda: to_low(s, c).wait_recv())
             last = planes - 1
             bottom = spreads(0, halo[s, c, 0], now[c, 0, rows, :], now[c, 1, rows, :])
             top = spreads(last, now[c, last - 1, rows, :], now[c, last, rows, :], halo[s, c, 1])
-            local = finish_plane(0, bottom) + finish_plane(last, top)
+            local = sum_all[c] + finish_plane(0, bottom) + finish_plane(last, top)
             if s < depth - 1:
                 send_halo(s + 1, c)
-
-            def inner(i, total_sum):
-                base = 1 + i * block
-                below = now[c, base - 1, rows, :]
-                center = now[c, base, rows, :]
-                waiting = None
-                for k in range(block):
-                    above = now[c, base + k + 1, rows, :]
-                    mixed = spreads(base + k, below, center, above)
-                    below, center = center, above
-                    if k:
-                        total_sum = total_sum + finish_plane(base + k - 1, waiting)
-                    waiting = mixed
-                return total_sum + finish_plane(base + block - 1, waiting)
-
-            local = lax.fori_loop(0, (planes - 2) // block, inner, local)
+            if s > 0:
+                local = run(s, c, 1, s, local)
+                local = run(s, c, last - s, s, local)
+            sum_all[c] = local
             if s == 0:
                 sum_first[c] = local
-                sum_all[c] = local
-            else:
-                sum_all[c] = sum_all[c] + local
             return carry
 
-        lax.fori_loop(0, classes, advance, 0)
-        if s == 0:
-            for shift in range(1, n_slab):
-                part_copy((slab + shift) % n_slab).start()
-
-    for shift in range(1, n_slab):
-        part_wait((slab + shift) % n_slab).wait_recv()
-    part_slots[slab] = sum_first[...]
-    length_sum = numbers[0]
-    for i in range(1, everyone):
-        length_sum = length_sum + numbers[i]
-    length_sum = tile(length_sum.astype(jnp.float32))
-    level = jnp.zeros((8, ny), jnp.float32)
-    for c in range(classes):
+        lax.fori_loop(0, classes, each, 0)
+
+    def scale_of(c, length_sum):
         whole = part_slots[0, c]
         for i in range(1, n_slab):
             whole = whole + part_slots[i, c]
         partition = tile(jnp.sum(whole)) / cells
-        fraction = tile(length_of(first + c)) / length_sum
-        scale = fraction * step_of(c) / partition
-        level = level + scale * sum_all[c]
-        for s in range(depth):
-            second = scale * kind_of(c, s).astype(jnp.float32)
-            weight[c, s, 0] = scale - second
-            weight[c, s, 1] = second
+        return tile(length_of(first + c)) / length_sum * step_of(c) / partition
+
+    def weigh():
+        for shift in range(1, n_slab):
+            part_wait((slab + shift) % n_slab).wait_recv()
+        part_slots[slab] = sum_first[...]
+        length_sum = numbers[0]
+        for i in range(1, everyone):
+            length_sum = length_sum + numbers[i]
+        length_sum = tile(length_sum.astype(jnp.float32))
+        for c in range(classes):
+            scale = scale_of(c, length_sum)
+            scales[c] = scale
+            for s in range(depth):
+                second = scale * kind_of(c, s).astype(jnp.float32)
+                weight[c, s, 0] = scale - second
+                weight[c, s, 1] = second
 
     lane_rows = dens.shape[0] // lanes
     lane_planes = planes // lanes
@@ -308,28 +324,35 @@
             src_ref=level_send.at[bits], dst_ref=level_slots.at[peer], send_sem=level_ssem.at[peer],
             recv_sem=level_rsem.at[peer], device_id=(me, peer), device_id_type=MESH)
 
-    level_send[0] = level
-    if bits:
-        tile_copy(0).start()
-
-    for lane in range(lanes):
-        def combine(z, carry):
-            one = jnp.zeros((groups, 8, ny), jnp.float32)
-            two = one
-            for c in range(classes):
-                for s in range(depth):
-                    value = as_tiles(product[s][c, z])
-                    one = one + weight[c, s, 0][None] * value
-                    two = two + weight[c, s, 1][None] * value
-            dens[at(z * 2 * nx, nx)] = one.reshape(nx, ny)
-            dens[at(z * 2 * nx + nx, nx)] = two.reshape(nx, ny)
-            return carry
-
+    def combine(z, carry):
+        one = jnp.zeros((groups, 8, ny), jnp.float32)
+        two = one
+        for c in range(classes):
+            for s in range(depth):
+                value = as_tiles(product[s][c, z])
+                one = one + weight[c, s, 0][None] * value
+                two = two + weight[c, s, 1][None] * value
+        dens[at(z * 2 * nx, nx)] = one.reshape(nx, ny)
+        dens[at(z * 2 * nx + nx, nx)] = two.reshape(nx, ny)
+        return carry
+
+    def start_lane(lane):
         lax.fori_loop(lane * lane_planes, (lane + 1) * lane_planes, combine, 0)
-        if bits:
-            reduce_copy(lane, 0).start()
-
-    for phase in range(bits):
+        reduce_copy(lane, 0).start()
+
+    def add(lane, phase):
+        reduce_copy(lane, phase).wait_recv()
+        start, size = window(lane, phase + 1)
+        into = lane * lane_rows + lane_rows - lane_rows // 2**phase
+        value = dens[at(start, size)] + received[pl.ds(into, size)]
+        if phase < bits - 1:
+            dens[at(start, size)] = value
+            reduce_copy(lane, phase + 1).start()
+        else:
+            full[at(start, size)] = value
+            gather_copy(lane, phase).start()
+
+    def add_tile(phase):
         tile_copy(phase).wait_recv()
         level_send[phase + 1] = level_send[phase] + level_recv[phase]
         if phase < bits - 1:
@@ -337,22 +360,61 @@
         else:
             for shift in range(1, n_slab):
                 level_copy((slab + shift) % n_slab).start()
-        for lane in range(lanes):
-            reduce_copy(lane, phase).wait_recv()
-            start, size = window(lane, phase + 1)
-            into = lane * lane_rows + lane_rows - lane_rows // 2**phase
-            value = dens[at(start, size)] + received[pl.ds(into, size)]
-            if phase < bits - 1:
-                dens[at(start, size)] = value
-                reduce_copy(lane, phase + 1).start()
-            else:
-                full[at(start, size)] = value
-                gather_copy(lane, phase).start()
-    for phase in reversed(range(bits)):
-        for lane in range(lanes):
-            gather_wait(lane, phase).wait_recv()
-            if phase > 0:
-                gather_copy(lane, phase - 1).start()
+
+    def gather(lane, phase):
+        gather_wait(lane, phase).wait_recv()
+        if phase > 0:
+            gather_copy(lane, phase - 1).start()
+
+    def events(group, with_tile):
+        def add_all(phase):
+            if with_tile:
+                add_tile(phase)
+            for lane in group:
+                add(lane, phase)
+
+        def gather_all(phase):
+            for lane in group:
+                gather(lane, phase)
+
+        return [functools.partial(add_all, p) for p in range(bits)] + [
+            functools.partial(gather_all, p) for p in reversed(range(bits))
+        ]
+
+    inner_lanes = list(range(1, lanes - 1))
+    outer_lanes = [0, lanes - 1]
+    inner_events = events(inner_lanes, False)
+    outer_events = events(outer_lanes, True)
+
+    middle(0)
+    ends(0)
+    for shift in range(1, n_slab):
+        part_copy((slab + shift) % n_slab).start()
+    for s in range(1, depth - 1):
+        middle(s)
+    ends(1)
+    middle(depth - 1)
+    weigh()
+    for lane in inner_lanes:
+        start_lane(lane)
+    for s in range(2, depth):
+        ends(s)
+        if s < depth - 1:
+            for event in inner_events[:2]:
+                event()
+    inner_events = inner_events[2:]
+
+    level = scales[0] * sum_all[0]
+    for c in range(1, classes):
+        level = level + scales[c] * sum_all[c]
+    level_send[0] = level
+    tile_copy(0).start()
+    for lane in outer_lanes:
+        start_lane(lane)
+    while len(outer_events) > 1:
+        if inner_events:
+            inner_events.pop(0)()
+        outer_events.pop(0)()
 
     for shift in range(1, n_slab):
         level_wait((slab + shift) % n_slab).wait_recv()
@@ -371,7 +433,10 @@
             fields_out[t, z] = (old + mixing * (flory_chi * other + pressure - old)).reshape(nx, ny)
         return carry
 
-    lax.fori_loop(0, planes, finish, 0)
+    lax.fori_loop(lane_planes, planes - lane_planes, finish, 0)
+    outer_events.pop(0)()
+    lax.fori_loop(0, lane_planes, finish, 0)
+    lax.fori_loop(planes - lane_planes, planes, finish, 0)
 
     for s in range(depth):
         def drain(c, carry, s=s):
@@ -394,7 +459,8 @@
     classes, depth, planes, nx, ny = q_back.shape
     lanes = 4
     bits = n_cls.bit_length() - 1
-    assert n_cls == 2**bits and n_slab > 1 and planes % lanes == 0
+    assert n_cls == 2**bits and bits > 1 and n_slab > 1
+    assert planes % lanes == 0 and planes // lanes >= depth > 2
     rows = planes * 2 * nx
     numbers = jnp.concatenate([lengths, steps_count, block_types.T.reshape(-1)])
     f32, bf16 = jnp.float32, jnp.bfloat16
@@ -418,6 +484,7 @@
             [pltpu.VMEM((classes, planes, nx + 2 * PAD, ny), f32)] * depth,
             pltpu.VMEM((depth, classes, 2, nx, ny), f32),
             [pltpu.VMEM((classes, planes, nx, ny), f32)] * depth,
+            pltpu.VMEM((classes, 8, ny), f32),
             pltpu.VMEM((classes, 8, ny), f32),
             pltpu.VMEM((classes, 8, ny), f32),
             pltpu.VMEM((classes, depth, 2, 8, ny), f32),

time: 46.9 us -> 45 us (0.959)
  Pallas kernels: 42.1 us -> 40.5 us
    pallas_call x1, Pallas kernels: 42.1 us -> 40.5 us  [body(): pl.pallas_call(functools.partial(kernel, n_cls, n_slab, lanes), out_shape...]
where the time goes in v3:
time: 45 us; the launch traced here: 44.6 us
  Pallas kernels  40.5 us (90%)
  local copies, waits for them, and re-layouts  2.71 us (6%)
  other arithmetic  0.75 us (2%)
  between operations  0.64 us (1%)
    pallas_call x1, Pallas kernels, body(): pl.pallas_call(functools.partial(kernel, n_cls, n_slab, lanes), out_shape...  40.5 us
    unnamed x2, local copies, waits for them, and re-layouts  1.94 us

profile of v3, /device:TPU:0, one launch (start us, length us, event | category | flops | bytes accessed | tf_op | source)
XLA Modules:
  0.0 44.6 jit_solution(11705366685286966231)
XLA Ops:
  0.6 0.8 %reshape.7 = s32[128]{0:T(128)S(1)} reshape(s32[4,32]{1,0:T(4,128)} %bitcast.1) | data formatting | bytes 1024 | tf_op jit(solution)/shard_map/reshape | solution.py:465
  1.4 0.7 %pad_add_fusion.numbers = s32[192]{0:T(256)S(1)} fusion(s32[128]{0:T(128)S(1)} %reshape.7, s32[32]{0:T(128)} %param.10, s32[32]{0:T(128)} %param.9), kind=kLoop, calls=%fused_computation | loop fusion | flops 384 | bytes 1536 | tf_op jit(solution)/shard_map/concatenate | solution.py:465
  2.1 40.5 %shard_map.77 = (f32[2,16,64,128]{3,2,1,0:T(8,128)S(1)}, bf16[4,16,64,128]{3,2,1,0:T(8,128)(2,1)S(1)}) custom-call(s32[192]{0:T(256)S(1)} %pad_add_fusion.numbers, bf16[4,16,64,128]{3,2,1,0:T(8,128)(2,1)} %q_init_hbm.1, bf16[4,4,16,64,128]{4,3,2,1,0:T(8,128)(2,1)} %q_back_hbm.1, f32[2,16,64,128]{3,2,1,0:T(8,128)} %fields_hbm.1), custom_call_target="tpu_custom_call" | custom-call | flops 41943040 | bytes 8388608 | tf_op jit(solution)/shard_map/pallas_call | solution.py:471
  42.7 1.0 %copy.10 = f32[2,16,64,128]{3,2,1,0:T(8,128)} copy(f32[2,16,64,128]{3,2,1,0:T(8,128)S(1)} %get-tuple-element.4) | data formatting | bytes 2097152
  43.7 1.0 %copy.11 = bf16[4,16,64,128]{3,2,1,0:T(8,128)(2,1)} copy(bf16[4,16,64,128]{3,2,1,0:T(8,128)(2,1)S(1)} %get-tuple-element.5) | data formatting | bytes 2097152

commit v4 on v3

--- a/solution.py
+++ b/solution.py
@@ -18,7 +18,7 @@
     n_cls, n_slab, lanes,
     numbers, q_init_hbm, q_back_hbm, fields_hbm,
     fields_out, q_out,
-    q_init, q_back, fields, half, weighted, halo, product, sum_first, sum_all, scales, weight,
+    q_init, q_back, fields, half, weighted, halo, product, sum_first, weight,
     part_slots, level_send, level_recv, level_slots, dens, received, full,
     load_sem, back_sem, halo_send, halo_recv, part_send, part_recv,
     reduce_send, reduce_recv, tile_send, tile_recv, level_ssem, level_rsem, gather_send, gather_recv,
@@ -51,7 +51,7 @@
     back_loads = [
         pltpu.make_async_copy(q_back_hbm.at[:, s], q_back.at[:, s], back_sem.at[s]) for s in range(depth)
     ]
-    for copy in loads + back_loads:
+    for copy in loads:
         copy.start()
 
     partners = [me + (1 - 2 * ((me // 2**b) % 2)) * 2**b for b in range(bits)]
@@ -118,6 +118,8 @@
 
     for copy in loads:
         copy.wait()
+    for copy in back_loads:
+        copy.start()
 
     def prepare_edges(c, carry):
         rate = (-0.5 * step_of(c))[None]
@@ -182,7 +184,7 @@
             else:
                 q_out[c, z] = forward.astype(jnp.bfloat16)
             product[s][c, z] = value
-            return jnp.sum(as_tiles(value), axis=0)
+            return jnp.sum(as_tiles(value), axis=0) if s == 0 else 0.0
 
         return spreads, finish_plane
 
@@ -202,15 +204,15 @@
         return total_sum + finish_plane(base + count - 1, waiting)
 
     def middle(s):
-        back_loads[s].wait()
         count = planes - 2 - 2 * s
         block = max(k for k in range(1, 8) if count % k == 0)
 
         def each(c, carry):
             local = lax.fori_loop(
                 0, count // block, lambda i, acc: run(s, c, s + 1 + i * block, block, acc),
-                jnp.zeros((8, ny), jnp.float32))
-            sum_all[c] = local if s == 0 else sum_all[c] + local
+                sum_first[c] if s == 0 else 0.0)
+            if s == 0:
+                sum_first[c] = local
             return carry
 
         lax.fori_loop(0, classes, each, 0)
@@ -224,14 +226,13 @@
             last = planes - 1
             bottom = spreads(0, halo[s, c, 0], now[c, 0, rows, :], now[c, 1, rows, :])
             top = spreads(last, now[c, last - 1, rows, :], now[c, last, rows, :], halo[s, c, 1])
-            local = sum_all[c] + finish_plane(0, bottom) + finish_plane(last, top)
+            local = finish_plane(0, bottom) + finish_plane(last, top)
             if s < depth - 1:
                 send_halo(s + 1, c)
             if s > 0:
-                local = run(s, c, 1, s, local)
-                local = run(s, c, last - s, s, local)
-            sum_all[c] = local
-            if s == 0:
+                run(s, c, 1, s, 0.0)
+                run(s, c, last - s, s, 0.0)
+            else:
                 sum_first[c] = local
             return carry
 
@@ -254,7 +255,6 @@
         length_sum = tile(length_sum.astype(jnp.float32))
         for c in range(classes):
             scale = scale_of(c, length_sum)
-            scales[c] = scale
             for s in range(depth):
                 second = scale * kind_of(c, s).astype(jnp.float32)
                 weight[c, s, 0] = scale - second
@@ -334,11 +334,12 @@
                 two = two + weight[c, s, 1][None] * value
         dens[at(z * 2 * nx, nx)] = one.reshape(nx, ny)
         dens[at(z * 2 * nx + nx, nx)] = two.reshape(nx, ny)
-        return carry
-
-    def start_lane(lane):
-        lax.fori_loop(lane * lane_planes, (lane + 1) * lane_planes, combine, 0)
+        return carry + jnp.sum(one + two, axis=0)
+
+    def start_lane(lane, total_sum):
+        total_sum = lax.fori_loop(lane * lane_planes, (lane + 1) * lane_planes, combine, total_sum)
         reduce_copy(lane, 0).start()
+        return total_sum
 
     def add(lane, phase):
         reduce_copy(lane, phase).wait_recv()
@@ -386,31 +387,34 @@
     inner_events = events(inner_lanes, False)
     outer_events = events(outer_lanes, True)
 
-    middle(0)
-    ends(0)
-    for shift in range(1, n_slab):
-        part_copy((slab + shift) % n_slab).start()
-    for s in range(1, depth - 1):
+    for s in range(depth - 1):
+        back_loads[s].wait()
+        ends(s)
         middle(s)
-    ends(1)
+        if s == 0:
+            for shift in range(1, n_slab):
+                part_copy((slab + shift) % n_slab).start()
+    back_loads[depth - 1].wait()
     middle(depth - 1)
     weigh()
+    level = jnp.zeros((8, ny), jnp.float32)
     for lane in inner_lanes:
-        start_lane(lane)
-    for s in range(2, depth):
-        ends(s)
-        if s < depth - 1:
-            for event in inner_events[:2]:
-                event()
-    inner_events = inner_events[2:]
-
-    level = scales[0] * sum_all[0]
-    for c in range(1, classes):
-        level = level + scales[c] * sum_all[c]
+        level = start_lane(lane, level)
+    ends(depth - 1)
+    inner_events.pop(0)()
+    for lane in outer_lanes:
+        level = start_lane(lane, level)
     level_send[0] = level
     tile_copy(0).start()
-    for lane in outer_lanes:
-        start_lane(lane)
+    for s in range(depth):
+        def drain(c, carry, s=s):
+            pl.when(has_low)(lambda: to_low(s, c).wait_send())
+            pl.when(has_high)(lambda: to_high(s, c).wait_send())
+            return carry
+
+        lax.fori_loop(0, classes, drain, 0)
+    for shift in range(1, n_slab):
+        part_copy((slab + shift) % n_slab).wait_send()
     while len(outer_events) > 1:
         if inner_events:
             inner_events.pop(0)()
@@ -434,25 +438,20 @@
         return carry
 
     lax.fori_loop(lane_planes, planes - lane_planes, finish, 0)
-    outer_events.pop(0)()
-    lax.fori_loop(0, lane_planes, finish, 0)
-    lax.fori_loop(planes - lane_planes, planes, finish, 0)
-
-    for s in range(depth):
-        def drain(c, carry, s=s):
-            pl.when(has_low)(lambda: to_low(s, c).wait_send())
-            pl.when(has_high)(lambda: to_high(s, c).wait_send())
-            return carry
-
-        lax.fori_loop(0, classes, drain, 0)
-    for shift in range(1, n_slab):
-        part_copy((slab + shift) % n_slab).wait_send()
-        level_copy((slab + shift) % n_slab).wait_send()
     for phase in range(bits):
         tile_copy(phase).wait_send()
         for lane in range(lanes):
             reduce_copy(lane, phase).wait_send()
-            gather_copy(lane, phase).wait_send()
+            if phase:
+                gather_copy(lane, phase).wait_send()
+    outer_events.pop(0)()
+    lax.fori_loop(0, lane_planes, finish, 0)
+    lax.fori_loop(planes - lane_planes, planes, finish, 0)
+
+    for shift in range(1, n_slab):
+        level_copy((slab + shift) % n_slab).wait_send()
+    for lane in range(lanes):
+        gather_copy(lane, 0).wait_send()
 
 
 def body(n_cls, n_slab, q_init, q_back, fields, lengths, steps_count, block_types):
@@ -484,8 +483,6 @@
             [pltpu.VMEM((classes, planes, nx + 2 * PAD, ny), f32)] * depth,
             pltpu.VMEM((depth, classes, 2, nx, ny), f32),
             [pltpu.VMEM((classes, planes, nx, ny), f32)] * depth,
-            pltpu.VMEM((classes, 8, ny), f32),
-            pltpu.VMEM((classes, 8, ny), f32),
             pltpu.VMEM((classes, 8, ny), f32),
             pltpu.VMEM((classes, depth, 2, 8, ny), f32),
             pltpu.VMEM((n_slab, classes, 8, ny), f32),

time: 45 us -> 46.9 us (1.042)
  Pallas kernels: 40.5 us -> 42.5 us
    pallas_call x1, Pallas kernels: 40.5 us -> 42.5 us  [body(): pl.pallas_call(functools.partial(kernel, n_cls, n_slab, lanes), out_shape...]
where the time goes in v4:
time: 46.9 us; the launch traced here: 46.6 us
  Pallas kernels  42.5 us (91%)
  local copies, waits for them, and re-layouts  2.71 us (6%)
  other arithmetic  0.75 us (2%)
  between operations  0.64 us (1%)
    pallas_call x1, Pallas kernels, body(): pl.pallas_call(functools.partial(kernel, n_cls, n_slab, lanes), out_shape...  42.5 us
    unnamed x2, local copies, waits for them, and re-layouts  1.94 us

profile of v4, /device:TPU:0, one launch (start us, length us, event | category | flops | bytes accessed | tf_op | source)
XLA Modules:
  0.0 46.6 jit_solution(15551863586396401240)
XLA Ops:
  0.6 0.8 %reshape.7 = s32[128]{0:T(128)S(1)} reshape(s32[4,32]{1,0:T(4,128)} %bitcast.1) | data formatting | bytes 1024 | tf_op jit(solution)/shard_map/reshape | solution.py:464
  1.4 0.7 %pad_add_fusion.numbers = s32[192]{0:T(256)S(1)} fusion(s32[128]{0:T(128)S(1)} %reshape.7, s32[32]{0:T(128)} %param.10, s32[32]{0:T(128)} %param.9), kind=kLoop, calls=%fused_computation | loop fusion | flops 384 | bytes 1536 | tf_op jit(solution)/shard_map/concatenate | solution.py:464
  2.1 42.5 %shard_map.77 = (f32[2,16,64,128]{3,2,1,0:T(8,128)S(1)}, bf16[4,16,64,128]{3,2,1,0:T(8,128)(2,1)S(1)}) custom-call(s32[192]{0:T(256)S(1)} %pad_add_fusion.numbers, bf16[4,16,64,128]{3,2,1,0:T(8,128)(2,1)} %q_init_hbm.1, bf16[4,4,16,64,128]{4,3,2,1,0:T(8,128)(2,1)} %q_back_hbm.1, f32[2,16,64,128]{3,2,1,0:T(8,128)} %fields_hbm.1), custom_call_target="tpu_custom_call" | custom-call | flops 41943040 | bytes 8388608 | tf_op jit(solution)/shard_map/pallas_call | solution.py:470
  44.7 1.0 %copy.10 = f32[2,16,64,128]{3,2,1,0:T(8,128)} copy(f32[2,16,64,128]{3,2,1,0:T(8,128)S(1)} %get-tuple-element.4) | data formatting | bytes 2097152
  45.7 1.0 %copy.11 = bf16[4,16,64,128]{3,2,1,0:T(8,128)(2,1)} copy(bf16[4,16,64,128]{3,2,1,0:T(8,128)(2,1)S(1)} %get-tuple-element.5) | data formatting | bytes 2097152

commit v5 on v4

--- a/solution.py
+++ b/solution.py
@@ -42,6 +42,8 @@
     cells = float(n_slab * planes * nx * ny)
     groups = nx // 8
     rows = pl.ds(PAD, nx)
+    before = PAD - 1 + me // n_cls
+    after = PAD + 1 + me // n_cls
     block = max(k for k in range(1, 8) if (planes - 2) % k == 0)
 
     loads = [
@@ -169,8 +171,8 @@
 
         def spreads(z, below, center, above):
             total = below + above
-            total = total + now[c, z, pl.ds(PAD - 1, nx), :]
-            total = total + now[c, z, pl.ds(PAD + 1, nx), :]
+            total = total + now[c, z, pl.ds(before, nx), :]
+            total = total + now[c, z, pl.ds(after, nx), :]
             total = as_tiles(total) + not_start * as_tiles(pltpu.roll(center, 1, 1))
             total = total + not_end * as_tiles(pltpu.roll(center, ny - 1, 1))
             return (keep * as_tiles(center) + spread * total).reshape(nx, ny)
@@ -210,7 +212,7 @@
         def each(c, carry):
             local = lax.fori_loop(
                 0, count // block, lambda i, acc: run(s, c, s + 1 + i * block, block, acc),
-                sum_first[c] if s == 0 else 0.0)
+                jnp.zeros((8, ny), jnp.float32) if s == 0 else 0.0)
             if s == 0:
                 sum_first[c] = local
             return carry
@@ -233,7 +235,7 @@
                 run(s, c, 1, s, 0.0)
                 run(s, c, last - s, s, 0.0)
             else:
-                sum_first[c] = local
+                sum_first[c] = sum_first[c] + local
             return carry
 
         lax.fori_loop(0, classes, each, 0)
@@ -387,20 +389,25 @@
     inner_events = events(inner_lanes, False)
     outer_events = events(outer_lanes, True)
 
-    for s in range(depth - 1):
+    back_loads[0].wait()
+    middle(0)
+    ends(0)
+    for shift in range(1, n_slab):
+        part_copy((slab + shift) % n_slab).start()
+    for s in range(1, depth - 1):
         back_loads[s].wait()
-        ends(s)
         middle(s)
-        if s == 0:
-            for shift in range(1, n_slab):
-                part_copy((slab + shift) % n_slab).start()
+    ends(1)
     back_loads[depth - 1].wait()
     middle(depth - 1)
     weigh()
     level = jnp.zeros((8, ny), jnp.float32)
     for lane in inner_lanes:
         level = start_lane(lane, level)
-    ends(depth - 1)
+    for s in range(2, depth):
+        ends(s)
+        if s < depth - 1:
+            inner_events.pop(0)()
     inner_events.pop(0)()
     for lane in outer_lanes:
         level = start_lane(lane, level)

time: 46.9 us -> 45.2 us (0.964)
  Pallas kernels: 42.5 us -> 40.8 us
    pallas_call x1, Pallas kernels: 42.5 us -> 40.8 us  [body(): pl.pallas_call(functools.partial(kernel, n_cls, n_slab, lanes), out_shape...]
where the time goes in v5:
time: 45.2 us; the launch traced here: 44.9 us
  Pallas kernels  40.8 us (90%)
  local copies, waits for them, and re-layouts  2.71 us (6%)
  other arithmetic  0.75 us (2%)
  between operations  0.64 us (1%)
    pallas_call x1, Pallas kernels, body(): pl.pallas_call(functools.partial(kernel, n_cls, n_slab, lanes), out_shape...  40.8 us
    unnamed x2, local copies, waits for them, and re-layouts  1.94 us

profile of v5, /device:TPU:0, one launch (start us, length us, event | category | flops | bytes accessed | tf_op | source)
XLA Modules:
  0.0 44.9 jit_solution(12083939208294696316)
XLA Ops:
  0.6 0.8 %reshape.7 = s32[128]{0:T(128)S(1)} reshape(s32[4,32]{1,0:T(4,128)} %bitcast.1) | data formatting | bytes 1024 | tf_op jit(solution)/shard_map/reshape | solution.py:471
  1.4 0.7 %pad_add_fusion.numbers = s32[192]{0:T(256)S(1)} fusion(s32[128]{0:T(128)S(1)} %reshape.7, s32[32]{0:T(128)} %param.10, s32[32]{0:T(128)} %param.9), kind=kLoop, calls=%fused_computation | loop fusion | flops 384 | bytes 1536 | tf_op jit(solution)/shard_map/concatenate | solution.py:471
  2.1 40.8 %shard_map.77 = (f32[2,16,64,128]{3,2,1,0:T(8,128)S(1)}, bf16[4,16,64,128]{3,2,1,0:T(8,128)(2,1)S(1)}) custom-call(s32[192]{0:T(256)S(1)} %pad_add_fusion.numbers, bf16[4,16,64,128]{3,2,1,0:T(8,128)(2,1)} %q_init_hbm.1, bf16[4,4,16,64,128]{4,3,2,1,0:T(8,128)(2,1)} %q_back_hbm.1, f32[2,16,64,128]{3,2,1,0:T(8,128)} %fields_hbm.1), custom_call_target="tpu_custom_call" | custom-call | flops 41943040 | bytes 8388608 | tf_op jit(solution)/shard_map/pallas_call | solution.py:477
  43.0 1.0 %copy.10 = f32[2,16,64,128]{3,2,1,0:T(8,128)} copy(f32[2,16,64,128]{3,2,1,0:T(8,128)S(1)} %get-tuple-element.4) | data formatting | bytes 2097152
  44.0 1.0 %copy.11 = bf16[4,16,64,128]{3,2,1,0:T(8,128)(2,1)} copy(bf16[4,16,64,128]{3,2,1,0:T(8,128)(2,1)S(1)} %get-tuple-element.5) | data formatting | bytes 2097152

commit v6 on v5

--- a/solution.py
+++ b/solution.py
@@ -27,13 +27,13 @@
     everyone = n_cls * classes
 
     def length_of(c):
-        return numbers[c].astype(jnp.float32)
+        return numbers[0, c].astype(jnp.float32)
 
     def count_of(c):
-        return numbers[everyone + c].astype(jnp.float32)
+        return numbers[1, c].astype(jnp.float32)
 
     def kind_of(c, s):
-        return numbers[2 * everyone + s * everyone + first + c]
+        return numbers[2 + s, first + c]
 
     me = lax.axis_index("cls")
     slab = lax.axis_index("slab")
@@ -251,9 +251,9 @@
         for shift in range(1, n_slab):
             part_wait((slab + shift) % n_slab).wait_recv()
         part_slots[slab] = sum_first[...]
-        length_sum = numbers[0]
+        length_sum = numbers[0, 0]
         for i in range(1, everyone):
-            length_sum = length_sum + numbers[i]
+            length_sum = length_sum + numbers[0, i]
         length_sum = tile(length_sum.astype(jnp.float32))
         for c in range(classes):
             scale = scale_of(c, length_sum)
@@ -394,21 +394,18 @@
     ends(0)
     for shift in range(1, n_slab):
         part_copy((slab + shift) % n_slab).start()
-    for s in range(1, depth - 1):
+    for s in range(1, depth):
         back_loads[s].wait()
         middle(s)
-    ends(1)
-    back_loads[depth - 1].wait()
-    middle(depth - 1)
     weigh()
     level = jnp.zeros((8, ny), jnp.float32)
     for lane in inner_lanes:
         level = start_lane(lane, level)
-    for s in range(2, depth):
+    for s in range(1, depth):
         ends(s)
-        if s < depth - 1:
-            inner_events.pop(0)()
-    inner_events.pop(0)()
+        for event in inner_events[:2 if s < depth - 1 else 0]:
+            event()
+            inner_events.pop(0)
     for lane in outer_lanes:
         level = start_lane(lane, level)
     level_send[0] = level
@@ -422,10 +419,11 @@
         lax.fori_loop(0, classes, drain, 0)
     for shift in range(1, n_slab):
         part_copy((slab + shift) % n_slab).wait_send()
-    while len(outer_events) > 1:
+    while len(outer_events) > 1 or inner_events:
         if inner_events:
             inner_events.pop(0)()
-        outer_events.pop(0)()
+        if len(outer_events) > 1:
+            outer_events.pop(0)()
 
     for shift in range(1, n_slab):
         level_wait((slab + shift) % n_slab).wait_recv()
@@ -461,6 +459,17 @@
         gather_copy(lane, 0).wait_send()
 
 
+def write_out(fields_new, q_final, fields_out, q_out, sem):
+    copies = [
+        pltpu.make_async_copy(fields_new, fields_out, sem.at[0]),
+        pltpu.make_async_copy(q_final, q_out, sem.at[1]),
+    ]
+    for copy in copies:
+        copy.start()
+    for copy in copies:
+        copy.wait()
+
+
 def body(n_cls, n_slab, q_init, q_back, fields, lengths, steps_count, block_types):
     classes, depth, planes, nx, ny = q_back.shape
     lanes = 4
@@ -468,13 +477,14 @@
     assert n_cls == 2**bits and bits > 1 and n_slab > 1
     assert planes % lanes == 0 and planes // lanes >= depth > 2
     rows = planes * 2 * nx
-    numbers = jnp.concatenate([lengths, steps_count, block_types.T.reshape(-1)])
+    numbers = jnp.concatenate([lengths[None], steps_count[None], block_types.T])
     f32, bf16 = jnp.float32, jnp.bfloat16
     dma = pltpu.SemaphoreType.DMA
     smem = pl.BlockSpec(memory_space=pltpu.SMEM)
     vmem = pl.BlockSpec(memory_space=pltpu.VMEM)
     hbm = pl.BlockSpec(memory_space=pltpu.HBM)
-    return pl.pallas_call(
+    hbm_any = pl.BlockSpec(memory_space=pl.ANY)
+    fields_new, q_final = pl.pallas_call(
         functools.partial(kernel, n_cls, n_slab, lanes),
         out_shape=(
             jax.ShapeDtypeStruct(fields.shape, f32),
@@ -521,6 +531,17 @@
             flops=20 * q_back.size, bytes_accessed=8 * 1024 * 1024, transcendentals=2 * q_init.size
         ),
     )(numbers, q_init, q_back, fields)
+    return pl.pallas_call(
+        write_out,
+        out_shape=(
+            jax.ShapeDtypeStruct(fields.shape, f32),
+            jax.ShapeDtypeStruct(q_init.shape, bf16),
+        ),
+        in_specs=[hbm_any, hbm_any],
+        out_specs=(hbm_any, hbm_any),
+        scratch_shapes=[dma((2,))],
+        cost_estimate=pl.CostEstimate(flops=0, bytes_accessed=4 * 1024 * 1024, transcendentals=0),
+    )(fields_new, q_final)
 
 
 def solution(mesh):

time: 45.2 us -> 113 us (2.50)
  Pallas kernels: 40.8 us -> 110 us
    pallas_call x0 -> x1, Pallas kernels: none -> 64.6 us  [body(): pl.pallas_call(write_out, out_shape=(jax.ShapeDtypeStruct(fields.shape, f...]
    pallas_call x1, Pallas kernels: 40.8 us -> 45.1 us  [body(): pl.pallas_call(functools.partial(kernel, n_cls, n_slab, lanes), out_shape...]
where the time goes in v6:
time: 113 us
  Pallas kernels  110 us (97%)
  local copies, waits for them, and re-layouts  1.98 us (2%)
    pallas_call x1, Pallas kernels, body(): pl.pallas_call(write_out, out_shape=(jax.ShapeDtypeStruct(fields.shape, f...  64.6 us
    pallas_call x1, Pallas kernels, body(): pl.pallas_call(functools.partial(kernel, n_cls, n_slab, lanes), out_shape...  45.1 us

profile of v6, /device:TPU:0, one launch (start us, length us, event | category | flops | bytes accessed | tf_op | source)
XLA Modules:
  0.0 113.1 jit_solution(17785009779131926110)
XLA Ops:
  0.6 0.7 pad_add_fusion.numbers
  1.3 45.1 %shard_map.77 = (f32[2,16,64,128]{3,2,1,0:T(8,128)S(1)}, bf16[4,16,64,128]{3,2,1,0:T(8,128)(2,1)S(1)}) custom-call(s32[6,32]{1,0:T(8,128)S(1)} %pad_add_fusion.numbers, bf16[4,16,64,128]{3,2,1,0:T(8,128)(2,1)} %q_init_hbm.1, bf16[4,4,16,64,128]{4,3,2,1,0:T(8,128)(2,1)} %q_back_hbm.1, f32[2,16,64,128]{3,2,1,0:T(8,128)} %fields_hbm.1), custom_call_target="tpu_custom_call" | custom-call | flops 41943040 | bytes 8388608 | tf_op jit(solution)/shard_map/pallas_call | solution.py:487
  46.5 0.0 copy-start
  46.5 1.0 copy-done
  47.5 0.0 copy-start.1
  47.5 1.0 copy-done.1
  48.5 64.6 %shard_map.78 = (f32[2,16,64,128]{3,2,1,0:T(8,128)}, bf16[4,16,64,128]{3,2,1,0:T(8,128)(2,1)}) custom-call(f32[2,16,64,128]{3,2,1,0:T(8,128)} %copy-done, bf16[4,16,64,128]{3,2,1,0:T(8,128)(2,1)} %copy-done.1), custom_call_target="tpu_custom_call" | custom-call | bytes 4194304 | tf_op jit(solution)/shard_map/pallas_call | solution.py:534
Async XLA Ops:
  46.5 1.0 copy-start
  47.5 1.0 copy-start.1

commit v7 on v6

--- a/solution.py
+++ b/solution.py
@@ -394,18 +394,21 @@
     ends(0)
     for shift in range(1, n_slab):
         part_copy((slab + shift) % n_slab).start()
-    for s in range(1, depth):
+    for s in range(1, depth - 1):
         back_loads[s].wait()
         middle(s)
+    ends(1)
+    back_loads[depth - 1].wait()
+    middle(depth - 1)
     weigh()
     level = jnp.zeros((8, ny), jnp.float32)
     for lane in inner_lanes:
         level = start_lane(lane, level)
-    for s in range(1, depth):
+    for s in range(2, depth):
         ends(s)
-        for event in inner_events[:2 if s < depth - 1 else 0]:
-            event()
-            inner_events.pop(0)
+        if s < depth - 1:
+            inner_events.pop(0)()
+    inner_events.pop(0)()
     for lane in outer_lanes:
         level = start_lane(lane, level)
     level_send[0] = level
@@ -537,7 +540,7 @@
             jax.ShapeDtypeStruct(fields.shape, f32),
             jax.ShapeDtypeStruct(q_init.shape, bf16),
         ),
-        in_specs=[hbm_any, hbm_any],
+        in_specs=[vmem, vmem],
         out_specs=(hbm_any, hbm_any),
         scratch_shapes=[dma((2,))],
         cost_estimate=pl.CostEstimate(flops=0, bytes_accessed=4 * 1024 * 1024, transcendentals=0),

time: 113 us -> 47.5 us (0.42)
  Pallas kernels: 110 us -> 43.9 us
    pallas_call x1, Pallas kernels: 64.6 us -> 2.87 us  [body(): pl.pallas_call(write_out, out_shape=(jax.ShapeDtypeStruct(fields.shape, f...]
    pallas_call x1, Pallas kernels: 45.1 us -> 41 us  [body(): pl.pallas_call(functools.partial(kernel, n_cls, n_slab, lanes), out_shape...]
where the time goes in v7:
time: 47.5 us; the launch traced here: 47.2 us
  Pallas kernels  43.9 us (92%)
  local copies, waits for them, and re-layouts  1.98 us (4%)
  other arithmetic  0.71 us (1%)
  between operations  0.65 us (1%)
    pallas_call x1, Pallas kernels, body(): pl.pallas_call(functools.partial(kernel, n_cls, n_slab, lanes), out_shape...  41 us
    pallas_call x1, Pallas kernels, body(): pl.pallas_call(write_out, out_shape=(jax.ShapeDtypeStruct(fields.shape, f...  2.87 us
    unnamed x4, local copies, waits for them, and re-layouts  1.98 us

profile of v7, /device:TPU:0, one launch (start us, length us, event | category | flops | bytes accessed | tf_op | source)
XLA Modules:
  0.0 47.2 jit_solution(18415648108161394490)
XLA Ops:
  0.6 0.7 %pad_add_fusion.numbers = s32[6,32]{1,0:T(8,128)S(1)} fusion(s32[4,32]{1,0:T(4,128)} %bitcast.3, s32[1,32]{1,0:T(1,128)} %bitcast.4, s32[1,32]{1,0:T(1,128)} %bitcast.5), kind=kLoop, calls=%fused_computation | loop fusion | flops 384 | bytes 1536 | tf_op jit(solution)/shard_map/concatenate | solution.py:483
  1.3 41.0 %shard_map.77 = (f32[2,16,64,128]{3,2,1,0:T(8,128)S(1)}, bf16[4,16,64,128]{3,2,1,0:T(8,128)(2,1)S(1)}) custom-call(s32[6,32]{1,0:T(8,128)S(1)} %pad_add_fusion.numbers, bf16[4,16,64,128]{3,2,1,0:T(8,128)(2,1)} %q_init_hbm.1, bf16[4,4,16,64,128]{4,3,2,1,0:T(8,128)(2,1)} %q_back_hbm.1, f32[2,16,64,128]{3,2,1,0:T(8,128)} %fields_hbm.1), custom_call_target="tpu_custom_call" | custom-call | flops 41943040 | bytes 8388608 | tf_op jit(solution)/shard_map/pallas_call | solution.py:490
  42.3 0.0 copy-start
  42.3 1.0 %copy-done = f32[2,16,64,128]{3,2,1,0:T(8,128)} copy-done((f32[2,16,64,128]{3,2,1,0:T(8,128)}, f32[2,16,64,128]{3,2,1,0:T(8,128)S(1)}, u32[]{:S(2)}) %copy-start) | copy-done | bytes 1048600
  43.3 0.0 copy-start.1
  43.3 1.0 %copy-done.1 = bf16[4,16,64,128]{3,2,1,0:T(8,128)(2,1)} copy-done((bf16[4,16,64,128]{3,2,1,0:T(8,128)(2,1)}, bf16[4,16,64,128]{3,2,1,0:T(8,128)(2,1)S(1)}, u32[]{:S(2)}) %copy-start.1) | copy-done | bytes 1048600
  44.3 2.9 %shard_map.78 = (f32[2,16,64,128]{3,2,1,0:T(8,128)}, bf16[4,16,64,128]{3,2,1,0:T(8,128)(2,1)}) custom-call(f32[2,16,64,128]{3,2,1,0:T(8,128)} %copy-done, bf16[4,16,64,128]{3,2,1,0:T(8,128)(2,1)} %copy-done.1), custom_call_target="tpu_custom_call" | custom-call | bytes 4194304 | tf_op jit(solution)/shard_map/pallas_call | solution.py:537
Async XLA Ops:
  42.3 1.0 %copy-start = (f32[2,16,64,128]{3,2,1,0:T(8,128)}, f32[2,16,64,128]{3,2,1,0:T(8,128)S(1)}, u32[]{:S(2)}) copy-start(f32[2,16,64,128]{3,2,1,0:T(8,128)S(1)} %get-tuple-element.4.fields_new) | copy-start | bytes 3145732
  43.3 1.0 %copy-start.1 = (bf16[4,16,64,128]{3,2,1,0:T(8,128)(2,1)}, bf16[4,16,64,128]{3,2,1,0:T(8,128)(2,1)S(1)}, u32[]{:S(2)}) copy-start(bf16[4,16,64,128]{3,2,1,0:T(8,128)(2,1)S(1)} %get-tuple-element.5.q_final) | copy-start | bytes 3145732
